TPU v7x, 256 devices: a whole 4x4x8 slice. The times are simulated.
256 devices in a mesh: dp: 8 (over x, core), expert: 32 (over z, y).
Axes of the slice: x: 4, y: 4, z: 8, core: 2. Of those that a mesh axis runs over, the one named last changes fastest.
Arguments:
- tokens: bfloat16 [2, 1536, 7168], P(None, 'expert'), may hold values from -6 to 6
- routes: int32 [2, 1536, 4], P(None, 'expert'), may hold values from 0 to 31, all different within a row; in each aligned block of 48 rows (0 to 47, 48 to 95, ..., all dimensions but the last counted through in order) at most 9 rows name the same one
- route_weights: float32 [2, 1536, 4], P(None, 'expert'), may hold values from 0.1 to 1
- domains: int32 [2, 1536], P(None, 'expert'), may hold values from 0 to 3
- gate_weight: bfloat16 [32, 7168, 2048], P('expert', None, 'dp'), may hold values from -0.0625 to 0.0625
- up_weight: bfloat16 [32, 7168, 2048], P('expert', None, 'dp'), may hold values from -0.0625 to 0.0625
- down_weight: bfloat16 [32, 2048, 7168], P('expert', 'dp'), may hold values from -0.1875 to 0.1875
- up_entry: bfloat16 [32, 7168, 128], P('expert', 'dp'), may hold values from -0.0625 to 0.0625
- up_exit: bfloat16 [32, 128, 2048], P('expert', None, 'dp'), may hold values from -1 to 1
- down_entry: bfloat16 [32, 2048, 128], P('expert', 'dp'), may hold values from -0.125 to 0.125
- down_exit: bfloat16 [32, 128, 7168], P('expert', None, 'dp'), may hold values from -1 to 1
Outputs:
- mixed: bfloat16 [2, 1536, 7168], P(None, 'expert', 'dp')
Inputs may be any that keep to these rules, and one draw needn't show every extreme that they name: `routes`: each row names 4 different experts. Among the 48 tokens of one index of expert in one step, no expert is named by more than 9 rows, a bound that some block reaches.
All inputs are finite; a program needn't handle non-finite values.
Results may differ from a plain program's by a relative error of at most 0.027.
Values may be sent and summed in bfloat16 or wider, within the bound.
A program may use at most 128 MiB of HBM per device.

v0:
```python
import jax
import jax.numpy as jnp
from jax import lax
from jax.sharding import PartitionSpec as P

TOP = 4
RANK = 32
DOMAINS = 4
STEPS = 2


def on_device(
    tokens,
    routes,
    route_weights,
    domains,
    gate_weight,
    up_weight,
    down_weight,
    up_entry,
    up_exit,
    down_entry,
    down_exit,
):
    experts = lax.axis_size("expert")
    group_count = lax.axis_size("dp")
    tok_rows = tokens.shape[1]
    model_width = tokens.shape[2]
    part_width = model_width // group_count
    capacity = (tok_rows * TOP * 3 + 2 * experts - 1) // (2 * experts)
    slot_count = experts * capacity
    column_start = lax.axis_index("dp") * part_width
    gate_local = gate_weight[0]
    up_local = up_weight[0]
    down_local = down_weight[0]
    up_enter = up_entry[0]
    up_leave = up_exit[0]
    down_enter = down_entry[0]
    down_leave = down_exit[0]
    results = []
    for step_index in range(STEPS):
        chosen = routes[step_index].reshape(-1)
        onehot = (chosen[:, None] == jnp.arange(experts, dtype=jnp.int32)[None, :]).astype(
            jnp.int32
        )
        slot_rank = jnp.sum((jnp.cumsum(onehot, axis=0) - onehot) * onehot, axis=1)
        target = chosen * capacity + slot_rank
        placed = (target[None, :] == jnp.arange(slot_count, dtype=jnp.int32)[:, None]).astype(
            jnp.bfloat16
        )
        spread = jnp.sum(placed.reshape(slot_count, tok_rows, TOP), axis=2)
        send_rows = jnp.dot(spread, tokens[step_index], preferred_element_type=jnp.float32).astype(
            jnp.bfloat16
        )
        send_rows = send_rows.reshape(experts, capacity, model_width)
        domain_hot = (
            domains[step_index][:, None] == jnp.arange(DOMAINS, dtype=jnp.int32)[None, :]
        ).astype(jnp.bfloat16)
        send_domain = jnp.dot(spread, domain_hot, preferred_element_type=jnp.float32).astype(
            jnp.bfloat16
        )
        send_domain = send_domain.reshape(experts, capacity, DOMAINS)
        arrived_rows, arrived_domain = (
            lax.all_to_all(send_rows, "expert", split_axis=0, concat_axis=0, tiled=True),
            lax.all_to_all(send_domain, "expert", split_axis=0, concat_axis=0, tiled=True),
        )
        routed = arrived_rows.reshape(slot_count, model_width)
        own_columns = lax.dynamic_slice_in_dim(routed, column_start, part_width, 1)
        gate_sum = jnp.dot(routed, gate_local, preferred_element_type=jnp.float32)
        up_base = jnp.dot(routed, up_local, preferred_element_type=jnp.float32)
        domain_mask = jnp.repeat(arrived_domain.reshape(slot_count, DOMAINS), RANK, axis=1).astype(
            jnp.float32
        )
        low_rank = lax.psum(
            jnp.dot(own_columns, up_enter, preferred_element_type=jnp.float32).astype(jnp.bfloat16),
            "dp",
        ).astype(jnp.float32)
        low_rank = (low_rank * domain_mask).astype(jnp.bfloat16)
        up_sum = up_base + jnp.dot(low_rank, up_leave, preferred_element_type=jnp.float32)
        hidden = (jax.nn.silu(gate_sum) * up_sum).astype(jnp.bfloat16)
        low_down = lax.psum(
            jnp.dot(hidden, down_enter, preferred_element_type=jnp.float32).astype(jnp.bfloat16),
            "dp",
        ).astype(jnp.float32)
        low_down = (low_down * domain_mask).astype(jnp.bfloat16)
        adapter = jnp.dot(low_down, down_leave, preferred_element_type=jnp.float32)
        partial_value = jnp.dot(hidden, down_local, preferred_element_type=jnp.float32)
        own_block = lax.dynamic_slice_in_dim(partial_value, column_start, part_width, 1) + adapter
        partial_value = lax.dynamic_update_slice_in_dim(partial_value, own_block, column_start, 1)
        rounded = partial_value.astype(jnp.bfloat16)
        pair_weight = route_weights[step_index].reshape(-1)
        summed = lax.psum_scatter(rounded, "dp", scatter_dimension=1, tiled=True).astype(
            jnp.float32
        )
        back_rows = lax.all_to_all(
            summed.reshape(experts, capacity, part_width).astype(jnp.bfloat16),
            "expert",
            split_axis=0,
            concat_axis=0,
            tiled=True,
        ).astype(jnp.float32)
        back_rows = back_rows.reshape(slot_count, part_width)
        picked = back_rows[target] * pair_weight[:, None]
        mixed_part = jnp.sum(picked.reshape(tok_rows, TOP, part_width), axis=1)
        results.append(mixed_part.astype(jnp.bfloat16))
    return jnp.stack(results)


def solution(mesh):
    in_specs = (
        P(None, "expert", None),
        P(None, "expert", None),
        P(None, "expert", None),
        P(None, "expert"),
        P("expert", None, "dp"),
        P("expert", None, "dp"),
        P("expert", "dp", None),
        P("expert", "dp", None),
        P("expert", None, "dp"),
        P("expert", "dp", None),
        P("expert", None, "dp"),
    )
    out_specs = P(None, "expert", "dp")
    return jax.shard_map(
        on_device, mesh=mesh, in_specs=in_specs, out_specs=out_specs, check_vma=False
    )
```

profile of v0, /device:TPU:40, one launch (start us, length us, event | category | flops | bytes accessed | tf_op | source)
XLA Modules:
  0.0 679.1 jit_solution(8748891543235345247)
XLA Ops:
  6.5 0.8 slice_bitcast_fusion.3
  7.3 0.7 fusion.44
  10.5 11.2 %all-to-all-start.1 = ((bf16[32,9,4]{1,2,0:T(4,128)(2,1)}), bf16[32,9,4]{1,2,0:T(4,128)(2,1)S(1)}, u32[]{:S(2)}, u32[]{:S(2)}) async-start(bf16[32,9,4]{1,2,0:T(4,128)(2,1)} %copy.64), calls=%async_computation.1 | async-start | bytes 65536 | tf_op jit(solution)/shard_map/all_to_all | solution.py:65
  24.2 5.3 all-to-all-done.1
  29.5 5.8 all-to-all-start.4
  35.4 4.3 convolution_convert_fusion
  39.6 6.4 reshape.207
  46.0 10.0 %all-to-all-start.3 = ((bf16[32,9,7168]{2,1,0:T(8,128)(2,1)}), bf16[32,9,7168]{2,1,0:T(8,128)(2,1)}, u32[]{:S(2)}, u32[]{:S(2)}) async-start(bf16[32,9,7168]{2,1,0:T(8,128)(2,1)} %reshape.207), calls=%async_computation.3 | async-start | bytes 14680064 | tf_op jit(solution)/shard_map/all_to_all | solution.py:64
  56.1 3.2 convolution_convert_fusion.1
  59.3 6.4 reshape.200
  65.7 150.8 %all-to-all-done.3 = bf16[32,9,7168]{2,1,0:T(8,128)(2,1)} async-done(((bf16[32,9,7168]{2,1,0:T(8,128)(2,1)}), bf16[32,9,7168]{2,1,0:T(8,128)(2,1)}, u32[]{:S(2)}, u32[]{:S(2)}) %all-to-all-start.3) | async-done | bytes 4128800 | tf_op jit(solution)/shard_map/all_to_all | solution.py:64
  216.5 7.7 %all-to-all-start = ((bf16[32,9,7168]{2,1,0:T(8,128)(2,1)}), bf16[32,9,7168]{2,1,0:T(8,128)(2,1)}, u32[]{:S(2)}, u32[]{:S(2)}) async-start(bf16[32,9,7168]{2,1,0:T(8,128)(2,1)} %reshape.200), calls=%async_computation | async-start | bytes 14680064 | tf_op jit(solution)/shard_map/all_to_all | solution.py:64
  225.2 6.4 reshape.208
  231.6 2.0 convolution_convert_fusion.2
  233.6 4.5 fusion.4
  238.1 147.1 %all-to-all-done = bf16[32,9,7168]{2,1,0:T(8,128)(2,1)} async-done(((bf16[32,9,7168]{2,1,0:T(8,128)(2,1)}), bf16[32,9,7168]{2,1,0:T(8,128)(2,1)}, u32[]{:S(2)}, u32[]{:S(2)}) %all-to-all-start) | async-done | bytes 4128800 | tf_op jit(solution)/shard_map/all_to_all | solution.py:64
  385.2 6.3 reshape.201
  391.5 2.0 convolution_convert_fusion.3
  393.4 4.7 fusion.6
  398.1 0.9 copy-done.8
  399.0 1.2 fusion.8
  400.5 4.5 fusion.10
  405.1 61.0 %all-reduce.9.cloned.1.call-done = (bf16[288,128]{1,0:T(8,128)(2,1)}, bf16[288,128]{1,0:T(8,128)(2,1)}) async-done(((bf16[288,128]{1,0:T(8,128)(2,1)}, bf16[288,128]{1,0:T(8,128)(2,1)}), (bf16[288,128]{1,0:T(8,128)(2,1)}, bf16[288,128]{1,0:T(8,128)(2,1)})) %all-reduce.9.cloned.1.call-update) | async-done | bytes 147472 | tf_op jit(solution)/shard_map/psum | solution.py:74
  466.1 1.1 fusion.17
  467.2 0.8 convolution_convert_fusion.4
  468.0 1.1 fusion.16
  469.1 0.8 convolution_convert_fusion.5
  470.0 6.5 fusion.2
  476.4 55.4 %all-reduce.7.cloned.1.call-done = (bf16[288,128]{1,0:T(8,128)(2,1)}, bf16[288,128]{1,0:T(8,128)(2,1)}) async-done(((bf16[288,128]{1,0:T(8,128)(2,1)}, bf16[288,128]{1,0:T(8,128)(2,1)}), (bf16[288,128]{1,0:T(8,128)(2,1)}, bf16[288,128]{1,0:T(8,128)(2,1)})) %all-reduce.7.cloned.1.call-update) | async-done | bytes 147472 | tf_op jit(solution)/shard_map/psum | solution.py:81
  531.8 2.6 fusion.13
  534.4 5.9 convert_element_type.154
  540.3 7.3 %copy.80 = bf16[288,7168]{0,1:T(8,128)(2,1)} copy(bf16[288,7168]{1,0:T(8,128)(2,1)} %convert_element_type.154) | data formatting | bytes 8257536
  547.7 3.3 fusion
  551.3 2.6 convert_element_type.172
  553.9 7.5 %copy.82 = bf16[288,7168]{0,1:T(8,128)(2,1)} copy(bf16[288,7168]{1,0:T(8,128)(2,1)} %convert_element_type.172) | data formatting | bytes 8257536
  561.4 28.3 %reduce-scatter.7.cloned.1.call-done = bf16[896,288]{1,0:T(8,128)(2,1)} async-done(((bf16[7168,288]{1,0:T(8,128)(2,1)}), bf16[896,288]{1,0:T(8,128)(2,1)}) %reduce-scatter.7.cloned.1.call-update) | async-done | bytes 516112
  589.7 1.4 copy.81
  591.1 1.1 convert_element_type.155
  592.3 10.0 %all-to-all-start.2 = ((bf16[32,9,896]{2,1,0:T(8,128)(2,1)}), bf16[32,9,896]{2,1,0:T(8,128)(2,1)S(1)}, u32[]{:S(2)}, u32[]{:S(2)}) async-start(bf16[32,9,896]{2,1,0:T(8,128)(2,1)} %convert_element_type.155), calls=%async_computation.2 | async-start | bytes 1835008 | tf_op jit(solution)/shard_map/all_to_all | solution.py:95
  602.3 32.9 %reduce-scatter.9.cloned.1.call-done = bf16[896,288]{1,0:T(8,128)(2,1)} async-done(((bf16[7168,288]{1,0:T(8,128)(2,1)}), bf16[896,288]{1,0:T(8,128)(2,1)}) %reduce-scatter.9.cloned.1.call-update) | async-done | bytes 516112
  635.2 1.4 copy.83
  636.5 1.2 convert_element_type.173
  637.7 10.1 %all-to-all-start.5 = ((bf16[32,9,896]{2,1,0:T(8,128)(2,1)}), bf16[32,9,896]{2,1,0:T(8,128)(2,1)S(1)}, u32[]{:S(2)}, u32[]{:S(2)}) async-start(bf16[32,9,896]{2,1,0:T(8,128)(2,1)} %convert_element_type.173), calls=%async_computation.5 | async-start | bytes 1835008 | tf_op jit(solution)/shard_map/all_to_all | solution.py:95
  648.5 1.0 gather_fusion
  649.4 1.0 gather.11
  650.5 19.0 %all-to-all-done.5 = bf16[32,9,896]{2,1,0:T(8,128)(2,1)S(1)} async-done(((bf16[32,9,896]{2,1,0:T(8,128)(2,1)}), bf16[32,9,896]{2,1,0:T(8,128)(2,1)S(1)}, u32[]{:S(2)}, u32[]{:S(2)}) %all-to-all-start.5) | async-done | bytes 516128 | tf_op jit(solution)/shard_map/all_to_all | solution.py:95
  669.7 1.0 gather_fusion.1
  671.9 0.7 pad_maximum_fusion
  (89 shorter events, 8.5 us)
Async XLA Ops:
  6.5 525.3 %copy-start = (bf16[1,128,896]{2,1,0:T(8,128)(2,1)S(1)}, bf16[1,128,896]{2,1,0:T(8,128)(2,1)}, u32[]{:S(2)}) copy-start(bf16[1,128,896]{2,1,0:T(8,128)(2,1)} %param.21) | copy-start | bytes 688132
  10.5 19.0 %all-to-all-start.1 = ((bf16[32,9,4]{1,2,0:T(4,128)(2,1)}), bf16[32,9,4]{1,2,0:T(4,128)(2,1)S(1)}, u32[]{:S(2)}, u32[]{:S(2)}) async-start(bf16[32,9,4]{1,2,0:T(4,128)(2,1)} %copy.64), calls=%async_computation.1 | async-start | bytes 65536 | tf_op jit(solution)/shard_map/all_to_all | solution.py:65
  29.5 16.5 %all-to-all-start.4 = ((bf16[32,9,4]{1,2,0:T(4,128)(2,1)}), bf16[32,9,4]{1,2,0:T(4,128)(2,1)S(1)}, u32[]{:S(2)}, u32[]{:S(2)}) async-start(bf16[32,9,4]{1,2,0:T(4,128)(2,1)} %copy.74), calls=%async_computation.4 | async-start | bytes 65536 | tf_op jit(solution)/shard_map/all_to_all | solution.py:65
  46.0 10.1 %copy-start.3 = (bf16[2,48,7168]{2,1,0:T(8,128)(2,1)S(1)}, bf16[2,48,7168]{2,1,0:T(8,128)(2,1)}, u32[]{:S(2)}) copy-start(bf16[2,48,7168]{2,1,0:T(8,128)(2,1)} %param.11) | copy-start | bytes 4128772
  46.0 170.4 %all-to-all-start.3 = ((bf16[32,9,7168]{2,1,0:T(8,128)(2,1)}), bf16[32,9,7168]{2,1,0:T(8,128)(2,1)}, u32[]{:S(2)}, u32[]{:S(2)}) async-start(bf16[32,9,7168]{2,1,0:T(8,128)(2,1)} %reshape.207), calls=%async_computation.3 | async-start | bytes 14680064 | tf_op jit(solution)/shard_map/all_to_all | solution.py:64
  216.5 168.7 %all-to-all-start = ((bf16[32,9,7168]{2,1,0:T(8,128)(2,1)}), bf16[32,9,7168]{2,1,0:T(8,128)(2,1)}, u32[]{:S(2)}, u32[]{:S(2)}) async-start(bf16[32,9,7168]{2,1,0:T(8,128)(2,1)} %reshape.200), calls=%async_computation | async-start | bytes 14680064 | tf_op jit(solution)/shard_map/all_to_all | solution.py:64
  224.1 241.9 %all-reduce.9.cloned.1.call-start = ((), (), s32[]{:S(2)}) async-start(), calls=%async_computation.11 | async-start | bytes 294912 | tf_op jit(solution)/shard_map/psum | solution.py:74
  225.2 6.5 copy-start.4
  393.4 4.7 copy-start.1
  393.4 5.6 copy-start.8
  400.3 65.8 %copy-start.9 = (bf16[1,128,256]{2,1,0:T(8,128)(2,1)S(1)}, bf16[1,128,256]{2,1,0:T(8,128)(2,1)}, u32[]{:S(2)}) copy-start(bf16[1,128,256]{2,1,0:T(8,128)(2,1)} %param.19) | copy-start | bytes 196612
  400.3 66.8 %copy-start.5 = (bf16[1,256,128]{2,1,0:T(8,128)(2,1)S(1)}, bf16[1,256,128]{2,1,0:T(8,128)(2,1)}, u32[]{:S(2)}) copy-start(bf16[1,256,128]{2,1,0:T(8,128)(2,1)} %param.20) | copy-start | bytes 196612
  400.3 131.5 %all-reduce.7.cloned.1.call-start = ((), (), s32[]{:S(2)}) async-start(), calls=%async_computation.10 | async-start | bytes 294912 | tf_op jit(solution)/shard_map/psum | solution.py:81
  469.9 119.8 %reduce-scatter.7.cloned.1.call-start = ((), (), s32[]{:S(2)}) async-start(), calls=%async_computation.8 | async-start | bytes 6193152
  547.7 3.3 copy-start.6
  547.7 87.5 %reduce-scatter.9.cloned.1.call-start = ((), (), s32[]{:S(2)}) async-start(), calls=%async_computation.9 | async-start | bytes 6193152
  591.1 56.7 %copy-start.7 = (f32[2,48,4]{1,2,0:T(4,128)S(1)}, f32[2,48,4]{1,2,0:T(4,128)}, u32[]{:S(2)}) copy-start(f32[2,48,4]{1,2,0:T(4,128)} %param.13) | copy-start | bytes 4612
  592.3 45.5 %all-to-all-start.2 = ((bf16[32,9,896]{2,1,0:T(8,128)(2,1)}), bf16[32,9,896]{2,1,0:T(8,128)(2,1)S(1)}, u32[]{:S(2)}, u32[]{:S(2)}) async-start(bf16[32,9,896]{2,1,0:T(8,128)(2,1)} %convert_element_type.155), calls=%async_computation.2 | async-start | bytes 1835008 | tf_op jit(solution)/shard_map/all_to_all | solution.py:95
  637.7 31.8 %all-to-all-start.5 = ((bf16[32,9,896]{2,1,0:T(8,128)(2,1)}), bf16[32,9,896]{2,1,0:T(8,128)(2,1)S(1)}, u32[]{:S(2)}, u32[]{:S(2)}) async-start(bf16[32,9,896]{2,1,0:T(8,128)(2,1)} %convert_element_type.173), calls=%async_computation.5 | async-start | bytes 1835008 | tf_op jit(solution)/shard_map/all_to_all | solution.py:95
  669.7 1.2 copy-start.2
Sparse Core Ops, SparseCore 0:
  400.4 65.6 all-reduce.8
  470.0 61.7 all-reduce.6
  547.8 41.8 reduce-scatter.6
  592.2 42.9 reduce-scatter.8
where the time goes:
time: 682 us; the launch traced here: 679 us
  waiting for transfers between devices  500 us (73%)
  local copies, waits for them, and re-layouts  55.3 us (8%)
  starting transfers between devices  55.2 us (8%)
  matrix products  43.2 us (6%)
  between operations  13.6 us (2%)
  other arithmetic  11.9 us (2%)
    all_to_all x2, waiting for transfers between devices, on_device(): lax.all_to_all(send_rows, 'expert', split_axis=0, concat_axis=0, tiled=True)  298 us
    unnamed x6, waiting for transfers between devices  61.2 us
    psum x1, waiting for transfers between devices, on_device(): lax.psum(jnp.dot(own_columns, up_enter, preferred_element_type=jnp.float3...  61 us
    psum x1, waiting for transfers between devices, on_device(): lax.psum(jnp.dot(hidden, down_enter, preferred_element_type=jnp.float32)....  55.4 us
    all_to_all x2, starting transfers between devices, on_device(): lax.all_to_all(summed.reshape(experts, capacity, part_width).astype(jnp.b...  20.1 us
    all_to_all x2, waiting for transfers between devices, on_device(): lax.all_to_all(summed.reshape(experts, capacity, part_width).astype(jnp.b...  19 us
    unnamed x26, local copies, waits for them, and re-layouts  18.7 us
    all_to_all x2, starting transfers between devices, on_device(): lax.all_to_all(send_rows, 'expert', split_axis=0, concat_axis=0, tiled=True)  17.7 us
  transfers between devices with their start and end apart: 10, of which 8 were waited for; matrix products, arithmetic and copies ran while one was open for 10% of the time, Pallas kernels for 0%

commit v1 on v0

v1 whole, which is shorter than its diff:
```python
import jax
import jax.numpy as jnp
from jax import lax
from jax.experimental import pallas as pl
from jax.experimental.pallas import tpu as pltpu
from jax.sharding import PartitionSpec as P

MESH = pl.DeviceIdType.MESH
F32 = jnp.float32
BF16 = jnp.bfloat16

TOP = 4
RANK = 32
DOMAINS = 4
STEPS = 2
TOK = 48
CAP = 9
EXPERTS = 32
D = 7168
FFL = 256
PART = 896
LOW = RANK * DOMAINS
NX, NY, NZ = 4, 4, 8
SLOT = STEPS * CAP
ROWS = NY * SLOT
PAD = 80
ALL = NZ * ROWS
HALF = ALL // 2
BLOCK = STEPS * TOK
CHUNKS = ((0, 256), (256, 256), (512, 256), (768, 128))
NC = len(CHUNKS)
W = 256


def dot(a, b):
    return jnp.dot(a, b, preferred_element_type=F32)


def kernel(
    tokens, table, domhot, gate, up, down, up_enter, up_leave, down_enter, down_leave,
    out,
    wgu, wd, g, tab, sel, selwt, zs, zr, xg, mask, acc, hid,
    sb, sr, ss, hr, tr, tp, vz, own, ys, yr,
    load_sem, ysend, yrecv, tsend, trecv, zsend, zrecv, xsend, xrecv,
    wsend, wrecv, bsend, brecv, hsend, hrecv, rsend, rrecv, vsend, vrecv, osend, orecv,
):
    dp = lax.axis_index("dp")
    ex = lax.axis_index("expert")
    x, core = dp // 2, dp % 2
    z, y = ex // NY, ex % NY
    sib = x * 2 + (1 - core)
    ip, im, io = (x + 1) % NX, (x + 3) % NX, (x + 2) % NX
    xp, xm, xo = ip * 2 + core, im * 2 + core, io * 2 + core

    def at_y(m):
        return z * NY + (y + m) % NY

    def at_z(k):
        return ((z + k) % NZ) * NY + y

    def send(src, dst, ssem, rsem, **where):
        return pltpu.make_async_remote_copy(
            src_ref=src, dst_ref=dst, send_sem=ssem, recv_sem=rsem,
            device_id=where, device_id_type=MESH,
        )

    barrier = pltpu.get_barrier_semaphore()
    for peer in (xp, xm, sib):
        pl.semaphore_signal(barrier, inc=1, device_id={"dp": peer}, device_id_type=MESH)
    for m in range(1, NY):
        pl.semaphore_signal(barrier, inc=1, device_id={"expert": at_y(m)}, device_id_type=MESH)
    for k in range(1, NZ):
        pl.semaphore_signal(barrier, inc=1, device_id={"expert": at_z(k)}, device_id_type=MESH)

    token_loads = []
    for c, (off, wide) in enumerate(CHUNKS):
        for s in range(STEPS):
            token_loads.append(
                pltpu.make_async_copy(
                    tokens.at[s, :, pl.ds(pl.multiple_of(dp * PART + off, 128), wide)],
                    g.at[c, 0, pl.ds(s * TOK, TOK), pl.ds(0, wide)],
                    load_sem.at[c * STEPS + s],
                )
            )
    token_loads.append(
        pltpu.make_async_copy(
            domhot, g.at[NC - 1, 0, pl.ds(0, BLOCK), pl.ds(128, 128)], load_sem.at[8]
        )
    )
    my_rows = pl.ds(pl.multiple_of(dp * PART, 128), PART)
    weight_loads = [
        pltpu.make_async_copy(up_enter, wgu.at[my_rows, pl.ds(512, LOW)], load_sem.at[9]),
        pltpu.make_async_copy(down_leave, wd.at[pl.ds(FFL, LOW), my_rows], load_sem.at[10]),
        pltpu.make_async_copy(gate, wgu.at[:, pl.ds(0, FFL)], load_sem.at[11]),
        pltpu.make_async_copy(up, wgu.at[:, pl.ds(FFL, FFL)], load_sem.at[12]),
        pltpu.make_async_copy(down, wd.at[pl.ds(0, FFL), :], load_sem.at[13]),
    ]
    for copy in token_loads + weight_loads:
        copy.start()
    for c in range(NC):
        for m in range(NY):
            g[c, m, BLOCK:, :] = jnp.zeros((128 - BLOCK, W), BF16)
    for cc in range(NC):
        for k in range(NZ):
            vz[cc, k, PAD:, :] = jnp.zeros((128 - PAD, W), BF16)
    pl.semaphore_wait(barrier, 13)

    def table_copy(m):
        return send(
            table.at[(y + m) % NY], tab.at[m], tsend.at[m], trecv.at[m], expert=at_y(m)
        )

    def y_copy(c, m):
        i = c * NY + m
        return send(
            g.at[c, 0, pl.ds(0, BLOCK)], g.at[c, m, pl.ds(0, BLOCK)],
            ysend.at[i], yrecv.at[i], expert=at_y(m),
        )

    for m in range(1, NY):
        table_copy(m).start()
    for copy in token_loads:
        copy.wait()
    for c in range(NC):
        for m in range(1, NY):
            y_copy(c, m).start()

    def spread(block, ssem, rsem, base, first, second):
        def near(kind, to, who):
            return send(block(who, 0), block(who, 0), ssem.at[base + kind], rsem.at[base + kind], dp=to)

        def far(kind, to, who):
            return send(
                block(who, kind - 2), block(who, kind - 2),
                ssem.at[base + kind], rsem.at[base + kind], dp=to,
            )

        if first:
            near(0, xp, dp).start()
            near(1, xm, dp).start()
            near(2, sib, dp).start()
        if second == "middle":
            near(0, xp, xm).wait_recv()
            far(3, xp, xm).start()
            near(5, sib, xm).start()
            near(1, xm, xp).wait_recv()
            far(4, xm, xp).start()
            near(6, sib, xp).start()
        if second == "end":
            far(3, xp, xo).wait_recv()
            far(4, xm, xo).wait_recv()
            near(7, sib, xo).start()
        if second == "all":
            for kind, step in ((2, 0), (5, 3), (6, 1), (7, 2)):
                near(kind, sib, ((x + step) % NX) * 2 + 1 - core).wait_recv()
        if second == "sent":
            for kind in (0, 1, 2, 5, 6, 7):
                near(kind, sib, dp).wait_send()
            far(3, xp, dp).wait_send()
            far(4, xm, dp).wait_send()

    def enter_block(who, part):
        start, size = ((0, PART), (0, PART // 2), (PART // 2, PART // 2))[part]
        return wgu.at[pl.ds(pl.multiple_of(who * PART + start, 64), size), pl.ds(512, LOW)]

    def leave_block(who, part):
        start, size = ((0, LOW), (0, LOW // 2), (LOW // 2, LOW // 2))[part]
        return wd.at[pl.ds(FFL + start, size), pl.ds(pl.multiple_of(who * PART, 128), PART)]

    def token_block(c):
        wide = CHUNKS[c][1]

        def block(who, part):
            start, size = ((0, ALL), (0, HALF), (HALF, HALF))[part]
            return xg.at[c, who, pl.ds(start, size), pl.ds(0, wide)]

        return block

    def weights(first, second):
        spread(enter_block, wsend, wrecv, 0, first, second)
        spread(leave_block, wsend, wrecv, 8, first, second)

    def gather(c, first, second):
        spread(token_block(c), xsend, xrecv, c * 8, first, second)

    weight_loads[0].wait()
    weight_loads[1].wait()
    weights(True, None)

    for m in range(1, NY):
        table_copy(m).wait_recv()

    def choose(k, carry):
        zd = (z + k) % NZ
        for m in range(NY):
            if m == 0:
                code, weight = table[y, pl.ds(zd, 1), :], table[y, pl.ds(NZ + zd, 1), :]
            else:
                code, weight = tab[m, pl.ds(zd, 1), :], tab[m, pl.ds(NZ + zd, 1), :]
            code = jnp.where(code >= 0.0, code + float(SLOT * m), -1.0)
            at = lax.broadcasted_iota(jnp.int32, (128, 128), 0).astype(F32) == code
            hot = jnp.where(at, 1.0, 0.0)
            sel[pl.ds(pl.multiple_of(k * PAD, 16), PAD), m * 128 : (m + 1) * 128] = hot[
                :PAD
            ].astype(BF16)
            selwt[m * 128 : (m + 1) * 128, pl.ds(pl.multiple_of(k * 128, 128), 128)] = (
                jnp.where(at, weight, 0.0).T.astype(BF16)
            )
        return carry

    lax.fori_loop(0, NZ, choose, 0)

    def z_copy(c, k):
        i = c * NZ + k
        return send(zs.at[c, k], zr.at[c, k], zsend.at[i], zrecv.at[i], expert=at_z(k))

    def stage_b(c):
        for m in range(1, NY):
            y_copy(c, m).wait_recv()
        rows = dot(sel[...], g[c].reshape(NY * 128, W)).astype(BF16).reshape(NZ, PAD, W)
        zs[c] = rows
        for k in range(1, NZ):
            z_copy(c, k).start()
        zr[c, 0] = rows[0]

    def stage_c(c):
        for k in range(1, NZ):
            z_copy(c, k).wait_recv()
        rows = zr[c].astype(F32)[:, :ROWS].reshape(ALL, W).astype(BF16)
        if c < NC - 1:
            xg[c, dp] = rows
        else:
            xg[c, dp, :, :128] = rows[:, :128]
            mask[...] = rows[:, 128:]
        gather(c, True, None)

    def stage_e(c):
        gather(c, False, "end")
        gather(c, False, "all")
        off, wide = CHUNKS[c]

        def part(shard, carry):
            depth = pl.ds(pl.multiple_of(shard * PART + off, 128), wide)
            term = dot(xg[c, shard, :, :wide], wgu[depth, :])
            acc[...] += term
            return carry

        lax.fori_loop(0, 2 * NX, part, 0)

    acc[...] = jnp.zeros_like(acc)
    stage_b(0)
    stage_b(1)
    weights(False, "middle")
    stage_c(0)
    stage_b(2)
    weights(False, "end")
    stage_c(1)
    gather(0, False, "middle")
    stage_b(3)
    stage_c(2)
    gather(1, False, "middle")
    weights(False, "all")
    for copy in weight_loads[2:]:
        copy.wait()
    stage_e(0)
    stage_c(3)
    gather(2, False, "middle")
    stage_e(1)
    gather(3, False, "middle")
    stage_e(2)
    stage_e(3)

    domain = mask[...].astype(F32)
    low = (acc[:, 2 * FFL :] * domain).astype(BF16)
    gated = acc[:, :FFL]
    upped = acc[:, FFL : 2 * FFL] + dot(low, up_leave[...])
    hidden = (gated / (1.0 + jnp.exp(-gated)) * upped).astype(BF16)
    hid[:, :FFL] = hidden
    hid[:, FFL:] = (dot(hidden, down_enter[...]) * domain).astype(BF16)

    def partial(cc, shard):
        off, wide = CHUNKS[cc]
        return dot(hid[...], wd[:, pl.ds(pl.multiple_of(shard * PART + off, 128), wide)])

    def b_copy(cc, i):
        wide = CHUNKS[cc][1]
        n = cc * NX + i
        return send(
            sb.at[cc, i, :, pl.ds(0, wide)], sr.at[cc, i, :, pl.ds(0, wide)],
            bsend.at[n], brecv.at[n], dp=sib,
        )

    def h_copy(cc, i):
        wide = CHUNKS[cc][1]
        n = cc * 2 + i
        return send(
            ss.at[cc, 2, pl.ds(i * HALF, HALF), pl.ds(0, wide)],
            hr.at[cc, i, :, pl.ds(0, wide)],
            hsend.at[n], hrecv.at[n], dp=(xp, xm)[i],
        )

    def r_copy(cc, i):
        wide = CHUNKS[cc][1]
        n = cc * 2 + i
        return send(
            ss.at[cc, i, :, pl.ds(0, wide)], tr.at[cc, i, :, pl.ds(0, wide)],
            rsend.at[n], rrecv.at[n], dp=(xp, xm)[i],
        )

    def v_copy(cc, k):
        wide = CHUNKS[cc][1]
        n = cc * NZ + k
        return send(
            tp.at[cc, k, :, pl.ds(0, wide)], vz.at[cc, k, pl.ds(0, PAD), pl.ds(0, wide)],
            vsend.at[n], vrecv.at[n], expert=at_z(NZ - k),
        )

    def o_copy(cc, m):
        wide = CHUNKS[cc][1]
        n = cc * NY + m
        return send(
            ys.at[cc, m, :, pl.ds(0, wide)], yr.at[cc, m, :, pl.ds(0, wide)],
            osend.at[n], orecv.at[n], expert=at_y(NY - m),
        )

    def paired(cc, i):
        wide = CHUNKS[cc][1]
        b_copy(cc, i).wait_recv()
        return partial(cc, i * 2 + core) + sr[cc, i, :, :wide].astype(F32)

    def stage_1(cc):
        wide = CHUNKS[cc][1]

        def one(j, carry):
            i = (x + 2 + j) % NX
            sb[cc, i, :, :wide] = partial(cc, i * 2 + 1 - core).astype(BF16)
            b_copy(cc, i).start()
            return carry

        lax.fori_loop(0, NX, one, 0)

    def stage_2(cc):
        ss[cc, 2, :, : CHUNKS[cc][1]] = paired(cc, io).astype(BF16)
        h_copy(cc, 0).start()
        h_copy(cc, 1).start()

    def stage_3(cc):
        wide = CHUNKS[cc][1]
        for i, to in enumerate((ip, im)):
            total = paired(cc, to)
            h_copy(cc, i).wait_recv()
            more = hr[cc, i, :, :wide].astype(F32)
            if i == 0:
                ss[cc, 0, :HALF, :wide] = (total[:HALF] + more).astype(BF16)
                ss[cc, 0, HALF:, :wide] = total[HALF:].astype(BF16)
            else:
                ss[cc, 1, :HALF, :wide] = total[:HALF].astype(BF16)
                ss[cc, 1, HALF:, :wide] = (total[HALF:] + more).astype(BF16)
            r_copy(cc, i).start()

    def stage_4(cc):
        wide = CHUNKS[cc][1]
        total = paired(cc, x)
        for i in range(2):
            r_copy(cc, i).wait_recv()
            total = total + tr[cc, i, :, :wide].astype(F32)
        total = total.reshape(NZ, ROWS, wide)
        total = jnp.concatenate([total, jnp.zeros((NZ, PAD - ROWS, wide), F32)], axis=1)
        rows = total.astype(BF16)
        tp[cc, :, :, :wide] = rows
        for k in range(1, NZ):
            v_copy(cc, k).start()
        vz[cc, 0, :PAD, :wide] = rows[0]

    def stage_5(cc):
        wide = CHUNKS[cc][1]
        for k in range(1, NZ):
            v_copy(cc, k).wait_recv()
        rows = vz[cc, :, :, :wide].reshape(NZ * 128, wide)
        mixed = dot(selwt[...], rows).reshape(NY, 128, wide)[:, :BLOCK]
        for m in range(1, NY):
            ys[cc, m, :, :wide] = mixed[m].astype(BF16)
            o_copy(cc, m).start()
        own[cc, :, :wide] = mixed[0]

    def stage_6(cc):
        off, wide = CHUNKS[cc]
        total = own[cc, :, :wide]
        for m in range(1, NY):
            o_copy(cc, m).wait_recv()
            total = total + yr[cc, m, :, :wide].astype(F32)
        total = total.astype(BF16)
        for s in range(STEPS):
            out[s, :, off : off + wide] = total[s * TOK : (s + 1) * TOK]

    stages = (stage_1, stage_2, stage_3, stage_4, stage_5, stage_6)
    for stage, cc in (
        (1, 0), (1, 1), (2, 0), (2, 1), (3, 0), (1, 2), (2, 2), (3, 1), (4, 0), (1, 3), (2, 3),
        (3, 2), (4, 1), (5, 0), (3, 3), (4, 2), (5, 1), (6, 0), (4, 3), (5, 2), (6, 1),
        (5, 3), (6, 2), (6, 3),
    ):
        stages[stage - 1](cc)

    for m in range(1, NY):
        table_copy(m).wait_send()
    weights(False, "sent")
    for c in range(NC):
        for m in range(1, NY):
            y_copy(c, m).wait_send()
            o_copy(c, m).wait_send()
        for k in range(1, NZ):
            z_copy(c, k).wait_send()
            v_copy(c, k).wait_send()
        gather(c, False, "sent")
        for i in range(NX):
            b_copy(c, i).wait_send()
        for i in range(2):
            h_copy(c, i).wait_send()
            r_copy(c, i).wait_send()


def on_device(
    tokens,
    routes,
    route_weights,
    domains,
    gate_weight,
    up_weight,
    down_weight,
    up_entry,
    up_exit,
    down_entry,
    down_exit,
):
    experts = jnp.arange(EXPERTS, dtype=jnp.int32)
    named = routes[:, None, :, :] == experts[None, :, None, None]
    hit = jnp.sum(named.astype(F32), axis=3)
    weight = jnp.sum(jnp.where(named, route_weights[:, None, :, :], 0.0), axis=3)
    before = (jnp.arange(TOK)[:, None] < jnp.arange(TOK)[None, :]).astype(F32)
    rank = jnp.einsum("set,tu->seu", hit, before, preferred_element_type=F32)
    step = jnp.arange(STEPS, dtype=F32)[:, None, None]
    code = jnp.where(hit > 0, step * CAP + rank, -1.0)

    def arranged(array, fill):
        flat = jnp.transpose(array, (1, 0, 2)).reshape(NZ, NY, BLOCK)
        flat = jnp.transpose(flat, (1, 0, 2))
        return jnp.pad(flat, ((0, 0), (0, 0), (0, 128 - BLOCK)), constant_values=fill)

    table = jnp.concatenate([arranged(code, -1.0), arranged(weight, 0.0)], axis=1)
    domhot = (
        domains.reshape(BLOCK)[:, None] == (jnp.arange(LOW, dtype=jnp.int32) // RANK)[None, :]
    ).astype(BF16)

    any_spec = pl.BlockSpec(memory_space=pl.ANY)
    vmem_spec = pl.BlockSpec(memory_space=pltpu.VMEM)
    dma = pltpu.SemaphoreType.DMA
    vmem = pltpu.VMEM
    return pl.pallas_call(
        kernel,
        out_shape=jax.ShapeDtypeStruct((STEPS, TOK, PART), BF16),
        in_specs=[any_spec, vmem_spec] + [any_spec] * 5 + [vmem_spec, vmem_spec, any_spec],
        out_specs=vmem_spec,
        scratch_shapes=[
            vmem((D, 2 * FFL + LOW), BF16),
            vmem((FFL + LOW, D), BF16),
            vmem((NC, NY, 128, W), BF16),
            vmem((NY, 2 * NZ, 128), F32),
            vmem((NZ * PAD, NY * 128), BF16),
            vmem((NY * 128, NZ * 128), BF16),
            vmem((NC, NZ, PAD, W), BF16),
            vmem((NC, NZ, PAD, W), BF16),
            vmem((NC, 2 * NX, ALL, W), BF16),
            vmem((ALL, LOW), BF16),
            vmem((ALL, 2 * FFL + LOW), F32),
            vmem((ALL, FFL + LOW), BF16),
            vmem((NC, NX, ALL, W), BF16),
            vmem((NC, NX, ALL, W), BF16),
            vmem((NC, 3, ALL, W), BF16),
            vmem((NC, 2, HALF, W), BF16),
            vmem((NC, 2, ALL, W), BF16),
            vmem((NC, NZ, PAD, W), BF16),
            vmem((NC, NZ, 128, W), BF16),
            vmem((NC, BLOCK, W), F32),
            vmem((NC, NY, BLOCK, W), BF16),
            vmem((NC, NY, BLOCK, W), BF16),
            dma((14,)),
            dma((NC * NY,)), dma((NC * NY,)),
            dma((NY,)), dma((NY,)),
            dma((NC * NZ,)), dma((NC * NZ,)),
            dma((NC * 8,)), dma((NC * 8,)),
            dma((16,)), dma((16,)),
            dma((NC * NX,)), dma((NC * NX,)),
            dma((NC * 2,)), dma((NC * 2,)),
            dma((NC * 2,)), dma((NC * 2,)),
            dma((NC * NZ,)), dma((NC * NZ,)),
            dma((NC * NY,)), dma((NC * NY,)),
        ],
        compiler_params=pltpu.CompilerParams(
            collective_id=0, has_side_effects=True, vmem_limit_bytes=62 * 1024 * 1024
        ),
        name="moe",
    )(
        tokens, table, domhot, gate_weight[0], up_weight[0], down_weight[0],
        up_entry[0], up_exit[0], down_entry[0], down_exit[0],
    )


def solution(mesh):
    in_specs = (
        P(None, "expert", None),
        P(None, "expert", None),
        P(None, "expert", None),
        P(None, "expert"),
        P("expert", None, "dp"),
        P("expert", None, "dp"),
        P("expert", "dp", None),
        P("expert", "dp", None),
        P("expert", None, "dp"),
        P("expert", "dp", None),
        P("expert", None, "dp"),
    )
    out_specs = P(None, "expert", "dp")
    return jax.shard_map(
        on_device, mesh=mesh, in_specs=in_specs, out_specs=out_specs, check_vma=False
    )
```

time: 682 us -> 130 us (0.19)
  waiting for transfers between devices: 500 us -> 0 us
  Pallas kernels: 0 us -> 125 us
  starting transfers between devices: 55.2 us -> 0 us
  local copies, waits for them, and re-layouts: 55.3 us -> 2.67 us
  matrix products: 43.2 us -> 0.07 us
  between operations: 13.6 us -> 0.03 us
  other arithmetic: 11.9 us -> 2.07 us
    all_to_all x6 -> x0, waiting for transfers between devices: 322 us -> none  [the longest x2 298 us: on_device(): lax.all_to_all(send_rows, 'expert', split_axis=0, concat_axis=0, tiled=True)]
    pallas_call x0 -> x1, Pallas kernels: none -> 125 us  [on_device(): pl.pallas_call(kernel, out_shape=jax.ShapeDtypeStruct((STEPS, TOK, PART),...]
    psum x2 -> x0, waiting for transfers between devices: 116 us -> none  [the longest x1 61 us: on_device(): lax.psum(jnp.dot(own_columns, up_enter, preferred_element_type=jnp.float3...]
    unnamed x6 -> x0, waiting for transfers between devices: 61.2 us -> none
    all_to_all x6 -> x0, starting transfers between devices: 54.9 us -> none  [the longest x2 20.1 us: on_device(): lax.all_to_all(summed.reshape(experts, capacity, part_width).astype(jnp.b...]
    dot_general x18 -> x1, matrix products: 43.2 us -> 0.07 us  [on_device(): rank = jnp.einsum('set,tu->seu', hit, before, preferred_element_type=F32)]
    reshape x10 -> x2, local copies, waits for them, and re-layouts: 27.4 us -> 0.19 us  [arranged(): flat = jnp.transpose(array, (1, 0, 2)).reshape(NZ, NY, BLOCK)]
    unnamed x26 -> x1, local copies, waits for them, and re-layouts: 18.7 us -> 1.6 us
  transfers between devices with their start and end apart: 10 -> 0, of which waited for: 8 -> 0; matrix products, arithmetic and copies ran while one was open for 10% -> 0% of each run, Pallas kernels for 0% -> 0%
where the time goes in v1:
time: 130 us
  Pallas kernels  125 us (96%)
  local copies, waits for them, and re-layouts  2.67 us (2%)
  other arithmetic  2.07 us (2%)
    pallas_call x1, Pallas kernels, on_device(): pl.pallas_call(kernel, out_shape=jax.ShapeDtypeStruct((STEPS, TOK, PART),...  125 us

profile of v1, /device:TPU:40, one launch (start us, length us, event | category | flops | bytes accessed | tf_op | source)
XLA Modules:
  0.0 130.1 jit_solution(9121937455895957340)
XLA Ops:
  0.0 0.8 eq.31
  0.8 0.7 compare_convert_fusion.domhot
  1.5 0.7 convert_reduce_fusion
  2.2 0.1 fusion.1
  2.3 0.1 copy.19
  2.4 0.1 reshape.27
  2.5 0.1 reshape.28
  2.6 0.6 select_maximum_fusion.table
  3.2 125.3 %moe.1 = bf16[2,48,896]{2,1,0:T(8,128)(2,1)} custom-call(bf16[2,48,7168]{2,1,0:T(8,128)(2,1)} %tokens.1, f32[4,16,128]{2,1,0:T(8,128)} %select_maximum_fusion.table, bf16[96,128]{1,0:T(8,128)(2,1)} %compare_convert_fusion.domhot, bf16[7168,256]{1,0:T(8,128)(2,1)} %bitcast.18, bf16[7168,256]{1,0:T(8,128)(2,1)} %bitcast.19, bf16[256,7168]{1,0:T(8,128)(2,1)} %bitcast.20, ...), custom_call_target="tpu_custom_call" | custom-call | tf_op jit(solution)/shard_map/moe/pallas_call | solution.py:458
  128.5 1.6 %copy.26 = bf16[2,48,896]{2,1,0:T(8,128)(2,1)} copy(bf16[2,48,896]{2,1,0:T(8,128)(2,1)} %moe.1) | data formatting | bytes 344064
  (4 shorter events, 0.0 us)

commit v2 on v0

v2 whole, which is shorter than its diff:
```python
import jax
import jax.numpy as jnp
from jax import lax
from jax.experimental import pallas as pl
from jax.experimental.pallas import tpu as pltpu
from jax.sharding import PartitionSpec as P

MESH = pl.DeviceIdType.MESH
F32 = jnp.float32
BF16 = jnp.bfloat16

TOP = 4
RANK = 32
DOMAINS = 4
STEPS = 2
TOK = 48
CAP = 9
EXPERTS = 32
D = 7168
FFL = 256
PART = 896
LOW = RANK * DOMAINS
NX, NY, NZ = 4, 4, 8
SLOT = STEPS * CAP
ROWS = NY * SLOT
PAD = 80
ALL = NZ * ROWS
BLOCK = STEPS * TOK
W = 256
OWN = ((0, 128), (128, 128), (256, 128), (384, 128), (512, 128), (640, 128), (768, 128))
NC = len(OWN)
AWAY = (0, 2, 6, 4, 1, 7, 3, 5)
NH = 2
WIDE = max(wide for _, wide in OWN)
HALF = ALL // NH
QUART = HALF // 2

ORDER = (
    "y4", "y6", "y1", "y3", "y0", "y5", "y2", "T", "B4", "B6", "B1", "B3", "b1", "b3", "b6", "b4", "B0", "B5", "B2",
    "C4.0", "b5", "b0", "b2", "C6.0", "C1.0", "D4.0", "C3.0", "C1.1", "D6.0", "C3.1", "D1.0", "e4.0", "C6.1", "E4.0",
    "D3.0", "C4.1", "D1.1", "e6.0", "E6.0", "D3.1", "e1.0", "C0.0", "E1.0", "D6.1", "C5.0", "e3.0", "E3.0", "D4.1",
    "C2.0", "L1.0", "e3.1", "e1.1", "C5.1", "L2.0", "D0.0", "E3.1", "e6.1", "E1.1", "E6.1", "D5.0", "e4.1", "C0.1",
    "E4.1", "D2.0", "C2.1", "L1.1", "D5.1", "L2.1", "L3.0", "e0.0", "e5.0", "E0.0", "E5.0", "D0.1", "e2.0", "E2.0",
    "H.0", "D2.1", "M1.0", "P6.0", "P0.0", "M2.0", "P3.0", "Q6.0", "Q0.0", "P1.0", "Q3.0", "P4.0", "P5.0", "Q1.0",
    "P2.0", "Q4.0", "Q5.0", "L3.1", "e5.1", "Q2.0", "e2.1", "R6.0", "M3.0", "R0.0", "e0.1", "E5.1", "R3.0", "R1.0",
    "R4.0", "E0.1", "R5.0", "R2.0", "E2.1", "H.1", "S6.0", "M1.1", "P5.1", "S0.0", "M2.1", "P3.1", "S3.0", "Q5.1",
    "P2.1", "Q3.1", "S1.0", "P4.1", "Q2.1", "P1.1", "S4.0", "Q4.1", "P6.1", "S5.0", "Q1.1", "P0.1", "Q6.1", "S2.0",
    "Q0.1", "M3.1", "R5.1", "R3.1", "R2.1", "R4.1", "R1.1", "R6.1", "R0.1", "S5.1", "S3.1", "S2.1", "S4.1", "S1.1",
    "U5", "S6.1", "U3", "S0.1", "U2", "U4", "V5", "U1", "V3", "U6", "V2", "U0", "V4", "V1", "V6", "V0",
)


def dot(a, b):
    return jnp.dot(a, b, preferred_element_type=F32)


def kernel(
    tokens, facts, gate, up, down, up_enter, up_leave, down_enter, down_leave,
    out,
    ws, wd, g, table, tab, sel, selwt, zs, zr, xs, mask, acc, hid,
    lp, lq, lx, lf, sb, sr, ss, hr, tr, tp, vz, own, ys, yr,
    load_sem, tsend, trecv, ysend, yrecv, zsend, zrecv, xsend, xrecv,
    lsend, lrecv, bsend, brecv, hsend, hrecv, rsend, rrecv, vsend, vrecv, osend, orecv,
):
    dp = lax.axis_index("dp")
    ex = lax.axis_index("expert")
    x, core = dp // 2, dp % 2
    z, y = ex // NY, ex % NY
    sib = x * 2 + (1 - core)
    ip, im, io = (x + 1) % NX, (x + 3) % NX, (x + 2) % NX
    xp, xm, xo = ip * 2 + core, im * 2 + core, io * 2 + core

    def at_x(i):
        return ((x + i) % NX) * 2 + core

    def at_y(m):
        return z * NY + (y + m) % NY

    def at_z(k):
        return ((z + k) % NZ) * NY + y

    def send(src, dst, ssem, rsem, **where):
        return pltpu.make_async_remote_copy(
            src_ref=src, dst_ref=dst, send_sem=ssem, recv_sem=rsem,
            device_id=where, device_id_type=MESH,
        )

    def lanes(index, wide):
        return pl.ds(pl.multiple_of(index * wide, wide), wide)

    barrier = pltpu.get_barrier_semaphore()
    for peer in (xp, xm, xo, sib):
        pl.semaphore_signal(barrier, inc=1, device_id={"dp": peer}, device_id_type=MESH)
    for m in range(1, NY):
        pl.semaphore_signal(barrier, inc=1, device_id={"expert": at_y(m)}, device_id_type=MESH)
    for k in range(1, NZ):
        pl.semaphore_signal(barrier, inc=1, device_id={"expert": at_z(k)}, device_id_type=MESH)

    loads = []
    for c, (off, wide) in enumerate(OWN):
        for s in range(STEPS):
            loads.append(
                (
                    tokens.at[s, :, pl.ds(pl.multiple_of(dp * PART + off, 128), wide)],
                    g.at[c, 0, pl.ds(s * TOK, TOK), pl.ds(0, wide)],
                )
            )
    n_tokens = len(loads)
    for c, (off, wide) in enumerate(OWN):
        for half, array in ((0, gate), (1, up)):
            cols = pl.ds(half * FFL, FFL)
            loads.append((array.at[:, pl.ds(off, wide), :], ws[c].at[:, :, cols]))
    loads.append((down, wd))
    loads = [pltpu.make_async_copy(a, b, load_sem.at[i]) for i, (a, b) in enumerate(loads)]
    for copy in loads:
        copy.start()
    for c in range(NC):
        for m in range(NY):
            g[c, m, BLOCK:, :] = jnp.zeros((128 - BLOCK, W), BF16)
        for k in range(NZ):
            vz[c, k, PAD:, :] = jnp.zeros((128 - PAD, WIDE), BF16)
    def count(shape, dim):
        return lax.broadcasted_iota(jnp.int32, shape, dim)

    row, token = count((EXPERTS, 128), 0), count((EXPERTS, 128), 1)
    expert = ((row % NZ) * NY + row // NZ).astype(F32)
    hit, weight = jnp.zeros((EXPERTS, 128), F32), jnp.zeros((EXPERTS, 128), F32)
    for k in range(TOP):
        named = (facts[k : k + 1, :] == expert) & (token < BLOCK)
        hit += jnp.where(named, 1.0, 0.0)
        weight += jnp.where(named, facts[TOP + k : TOP + k + 1, :], 0.0)
    first, second = count((128, 128), 0), count((128, 128), 1)
    before = (first < second) & ((first >= TOK) == (second >= TOK))
    rank = dot(hit.astype(BF16), jnp.where(before, 1.0, 0.0).astype(BF16))
    code = jnp.where(hit > 0.0, rank + jnp.where(token >= TOK, float(CAP), 0.0), -1.0)
    table[:, :NZ, :] = code.reshape(NY, NZ, 128)
    table[:, NZ:, :] = weight.reshape(NY, NZ, 128)
    domain = facts[2 * TOP : 2 * TOP + 1, :] == (first // RANK).astype(F32)
    g[0, 0, :BLOCK, 128:] = jnp.where(domain, 1.0, 0.0).T[:BLOCK].astype(BF16)
    pl.semaphore_wait(barrier, 14)

    def table_copy(m):
        return send(
            table.at[(y + m) % NY], tab.at[m], tsend.at[m], trecv.at[m], expert=at_y(m)
        )

    def y_copy(c, m):
        i, cols = c * NY + m, pl.ds(0, W if c == 0 else OWN[c][1])
        return send(
            g.at[c, 0, pl.ds(0, BLOCK), cols], g.at[c, m, pl.ds(0, BLOCK), cols],
            ysend.at[i], yrecv.at[i], expert=at_y(m),
        )

    def stage_tables():
        for m in range(1, NY):
            table_copy(m).wait_recv()

        def choose(m, carry):
            for n, k in enumerate(AWAY):
                zd = (z + k) % NZ
                code, weight = tab[m, pl.ds(zd, 1), :], tab[m, pl.ds(NZ + zd, 1), :]
                code = jnp.where(code >= 0.0, code + (m * SLOT).astype(F32), -1.0)
                at = lax.broadcasted_iota(jnp.int32, (128, 128), 0).astype(F32) == code
                hot = jnp.where(at, 1.0, 0.0)[:PAD].astype(BF16)
                cols = pl.ds(pl.multiple_of(m * 128, 128), 128)
                sel[n * PAD : (n + 1) * PAD, cols] = hot
                selwt[cols, n * 128 : (n + 1) * 128] = jnp.where(at, weight, 0.0).T.astype(BF16)
            return carry

        lax.fori_loop(0, NY, choose, 0)

    def z_copy(c, n):
        i = c * NZ + n
        cols = pl.ds(0, W if c == 0 else OWN[c][1])
        return send(
            zs.at[c, n, :, cols], zr.at[c, n, :, cols], zsend.at[i], zrecv.at[i],
            expert=at_z(AWAY[n]),
        )

    def of_half(h):
        return [n for n in range(4 * h, 4 * h + 4) if n > 0]

    def stage_y(c):
        for copy in loads[c * STEPS : (c + 1) * STEPS]:
            copy.wait()
        for m in range(1, NY):
            y_copy(c, m).start()

    def stage_b(c):
        for m in range(1, NY):
            y_copy(c, m).wait_recv()
        take = W if c == 0 else OWN[c][1]
        rows = dot(sel[...], g[c, :, :, :take].reshape(NY * 128, take))
        rows = rows.astype(BF16).reshape(NZ, PAD, take)
        zs[c, :, :, :take] = rows
        for n in of_half(0):
            z_copy(c, n).start()
        zr[c, 0, :, :take] = rows[0]

    def stage_b2(c):
        for n in of_half(1):
            z_copy(c, n).start()

    def near(c, h, kind, to, who):
        n = (c * NH + h) * 8 + kind
        block = xs[c].at[pl.ds(h * HALF, HALF), lanes(who, OWN[c][1])]
        return send(block, block, xsend.at[n], xrecv.at[n], dp=to)

    def far(c, h, kind, to, who):
        n = (c * NH + h) * 8 + kind
        block = xs[c].at[pl.ds(h * HALF + (kind - 3) * QUART, QUART), lanes(who, OWN[c][1])]
        return send(block, block, xsend.at[n], xrecv.at[n], dp=to)

    def stage_c(c, h):
        for n in of_half(h):
            z_copy(c, n).wait_recv()
        wide, mine = OWN[c][1], slice(h * HALF, (h + 1) * HALF)
        take = W if c == 0 else wide
        rows = zr[c, 4 * h : 4 * h + 4, :, :take].astype(F32)[:, :ROWS]
        rows = rows.reshape(HALF, take).astype(BF16)
        xs[c][mine, lanes(dp, wide)] = rows[:, :wide]
        if c == 0:
            mask[mine, :] = rows[:, 128:]
        near(c, h, 0, xp, dp).start()
        near(c, h, 1, xm, dp).start()
        near(c, h, 2, sib, dp).start()

    def stage_d(c, h):
        near(c, h, 0, xp, xm).wait_recv()
        far(c, h, 3, xp, xm).start()
        near(c, h, 5, sib, xm).start()
        near(c, h, 1, xm, xp).wait_recv()
        far(c, h, 4, xm, xp).start()
        near(c, h, 6, sib, xp).start()

    started = [False] * NH

    def stage_e(c, h):
        far(c, h, 3, xp, xo).wait_recv()
        far(c, h, 4, xm, xo).wait_recv()
        near(c, h, 7, sib, xo).start()

    loaded = set()

    def stage_e2(c, h):
        for kind, step in ((2, 0), (5, 3), (6, 1), (7, 2)):
            near(c, h, kind, sib, ((x + step) % NX) * 2 + 1 - core).wait_recv()
        if c not in loaded:
            loaded.add(c)
            for half in range(2):
                loads[n_tokens + c * 2 + half].wait()
        mine, wide = slice(h * HALF, (h + 1) * HALF), OWN[c][1]
        term = dot(xs[c][mine, :], ws[c][...].reshape(8 * wide, 2 * FFL))
        if started[h]:
            acc[mine, :] += term
        else:
            acc[mine, :] = term
            started[h] = True

    def pair_copy(q, h):
        n = (q * NH + h) * 8
        away = pl.ds(pl.multiple_of(h * HALF + (1 - core) * QUART, 16), QUART)
        return send(lp.at[q, away], lq.at[q, h], lsend.at[n], lrecv.at[n], dp=sib)

    def low_copy(q, h, j):
        n = (q * NH + h) * 8 + j
        return send(lx.at[q, h, 0], lx.at[q, h, j], lsend.at[n], lrecv.at[n], dp=at_x(j))

    def back_copy(q, h, whose):
        n = (q * NH + h) * 8 + 4
        rows = lf.at[q, pl.ds(pl.multiple_of(h * HALF + whose * QUART, 16), QUART)]
        return send(rows, rows, lsend.at[n], lrecv.at[n], dp=sib)

    def stage_low(s, q, h):
        mine = slice(h * HALF, (h + 1) * HALF)
        home = pl.ds(pl.multiple_of(h * HALF + core * QUART, 16), QUART)
        if s == 1:
            if q == 0:
                total = jnp.zeros((HALF, LOW), F32)
                for c, (off, wide) in enumerate(OWN):
                    block = xs[c][mine, lanes(dp, wide)]
                    total += dot(block, up_enter[off : off + wide, :])
            else:
                total = dot(hid[mine, :], down_enter[...])
            lp[q, mine, :] = total.astype(BF16)
            pair_copy(q, h).start()
        elif s == 2:
            pair_copy(q, h).wait_recv()
            lx[q, h, 0] = (lp[q, home, :].astype(F32) + lq[q, h].astype(F32)).astype(BF16)
            for j in range(1, NX):
                low_copy(q, h, j).start()
        elif s == 3:
            total = lx[q, h, 0].astype(F32)
            for j in range(1, NX):
                low_copy(q, h, j).wait_recv()
                total += lx[q, h, j].astype(F32)
            lf[q, home, :] = (total * mask[home, :].astype(F32)).astype(BF16)
            back_copy(q, h, core).start()

    def stage_hidden(h):
        mine = slice(h * HALF, (h + 1) * HALF)
        back_copy(0, h, 1 - core).wait_recv()
        gated = acc[mine, :FFL]
        upped = acc[mine, FFL:] + dot(lf[0, mine, :], up_leave[...])
        hid[mine, :] = (gated / (1.0 + jnp.exp(-gated)) * upped).astype(BF16)
        if "down" not in loaded:
            loaded.add("down")
            loads[-1].wait()

    def partial(c, h, shard):
        off, wide = OWN[c]
        cols = pl.ds(pl.multiple_of(shard * PART + off, 128), wide)
        return dot(hid[h * HALF : (h + 1) * HALF, :], wd[:, cols])

    def b_copy(c, h, i):
        cols, n = pl.ds(0, OWN[c][1]), (c * NH + h) * NX + i
        rows = pl.ds(h * HALF, HALF)
        return send(
            sb.at[c, i, rows, cols], sr.at[c, i, rows, cols], bsend.at[n], brecv.at[n], dp=sib
        )

    def paired(c, h, i):
        b_copy(c, h, i).wait_recv()
        more = sr[c, i, h * HALF : (h + 1) * HALF, : OWN[c][1]].astype(F32)
        return partial(c, h, i * 2 + core) + more

    def h_copy(c, h, i):
        cols, n = pl.ds(0, OWN[c][1]), (c * NH + h) * 2 + i
        return send(
            ss.at[c, h, 2, pl.ds(i * QUART, QUART), cols], hr.at[c, h, i, :, cols],
            hsend.at[n], hrecv.at[n], dp=(xp, xm)[i],
        )

    def r_copy(c, h, i):
        cols, n = pl.ds(0, OWN[c][1]), (c * NH + h) * 2 + i
        return send(
            ss.at[c, h, i, :, cols], tr.at[c, h, i, :, cols],
            rsend.at[n], rrecv.at[n], dp=(xp, xm)[i],
        )

    def v_copy(c, n):
        cols, i = pl.ds(0, OWN[c][1]), c * NZ + n
        return send(
            tp.at[c, n, :, cols], vz.at[c, n, pl.ds(0, PAD), cols],
            vsend.at[i], vrecv.at[i], expert=at_z(NZ - AWAY[n]),
        )

    def o_copy(c, m):
        cols, n = pl.ds(0, OWN[c][1]), c * NY + m
        return send(
            ys.at[c, m, :, cols], yr.at[c, m, :, cols], osend.at[n], orecv.at[n],
            expert=at_y(NY - m),
        )

    def stage_1(c, h):
        wide = OWN[c][1]

        def one(j, carry):
            i = (x + 2 + j) % NX
            term = partial(c, h, i * 2 + 1 - core)
            sb[c, i, h * HALF : (h + 1) * HALF, :wide] = term.astype(BF16)
            b_copy(c, h, i).start()
            return carry

        lax.fori_loop(0, NX, one, 0)

    def stage_2(c, h):
        ss[c, h, 2, :, : OWN[c][1]] = paired(c, h, io).astype(BF16)
        h_copy(c, h, 0).start()
        h_copy(c, h, 1).start()

    def stage_3(c, h):
        wide = OWN[c][1]
        for i, to in enumerate((ip, im)):
            total = paired(c, h, to)
            h_copy(c, h, i).wait_recv()
            more = hr[c, h, i, :, :wide].astype(F32)
            if i == 0:
                ss[c, h, 0, :QUART, :wide] = (total[:QUART] + more).astype(BF16)
                ss[c, h, 0, QUART:, :wide] = total[QUART:].astype(BF16)
            else:
                ss[c, h, 1, :QUART, :wide] = total[:QUART].astype(BF16)
                ss[c, h, 1, QUART:, :wide] = (total[QUART:] + more).astype(BF16)
            r_copy(c, h, i).start()

    def stage_4(c, h):
        off, wide = OWN[c]
        if ("low", h) not in loaded:
            loaded.add(("low", h))
            back_copy(1, h, 1 - core).wait_recv()
        total = paired(c, h, x)
        total += dot(lf[1, h * HALF : (h + 1) * HALF, :], down_leave[:, off : off + wide])
        for i in range(2):
            r_copy(c, h, i).wait_recv()
            total += tr[c, h, i, :, :wide].astype(F32)
        total = total.reshape(4, ROWS, wide)
        total = jnp.concatenate([total, jnp.zeros((4, PAD - ROWS, wide), F32)], axis=1)
        rows = total.astype(BF16)
        tp[c, 4 * h : 4 * h + 4, :, :wide] = rows
        for n in of_half(h):
            v_copy(c, n).start()
        if h == 0:
            vz[c, 0, :PAD, :wide] = rows[0]

    def stage_5(c):
        wide = OWN[c][1]
        for n in range(1, NZ):
            v_copy(c, n).wait_recv()
        rows = vz[c, :, :, :wide].reshape(NZ * 128, wide)
        mixed = dot(selwt[...], rows).reshape(NY, 128, wide)[:, :BLOCK]
        for m in range(1, NY):
            ys[c, m, :, :wide] = mixed[m].astype(BF16)
            o_copy(c, m).start()
        own[c, :, :wide] = mixed[0]

    def stage_6(c):
        off, wide = OWN[c]
        total = own[c, :, :wide]
        for m in range(1, NY):
            o_copy(c, m).wait_recv()
            total += yr[c, m, :, :wide].astype(F32)
        total = total.astype(BF16)
        for s in range(STEPS):
            out[s, :, off : off + wide] = total[s * TOK : (s + 1) * TOK]

    for m in range(1, NY):
        table_copy(m).start()
    tab[0] = table[y]
    stages = {
        "T": stage_tables, "y": stage_y, "B": stage_b, "b": stage_b2, "C": stage_c, "D": stage_d,
        "e": stage_e, "E": stage_e2, "H": stage_hidden, "P": stage_1, "Q": stage_2, "R": stage_3,
        "S": stage_4, "U": stage_5, "V": stage_6,
    }
    def sent_out(c):
        for m in range(1, NY):
            y_copy(c, m).wait_send()
        for n in range(1, NZ):
            z_copy(c, n).wait_send()
        for h in range(NH):
            for kind in (0, 1, 2, 5, 6, 7):
                near(c, h, kind, sib, dp).wait_send()
            for i in range(2):
                far(c, h, 3 + i, xp, dp).wait_send()

    def sent_back():
        for m in range(1, NY):
            table_copy(m).wait_send()
        for h in range(NH):
            for q in range(2):
                pair_copy(q, h).wait_send()
                back_copy(q, h, core).wait_send()
                for j in range(1, NX):
                    low_copy(q, h, j).wait_send()
            for c in range(NC):
                for i in range(2):
                    h_copy(c, h, i).wait_send()
                    r_copy(c, h, i).wait_send()
                for i in range(NX):
                    b_copy(c, h, i).wait_send()
        for c in range(NC):
            for n in range(1, NZ):
                v_copy(c, n).wait_send()

    mixes = 0
    for name in ORDER:
        if name[0] == "U":
            sent_out(mixes)
            mixes += 1
            if mixes == NC:
                sent_back()
        numbers = [int(n) for n in name[1:].split(".") if n]
        if name[0] in "LM":
            stage_low(numbers[0], "LM".index(name[0]), numbers[1])
        else:
            stages[name[0]](*numbers)

    for c in range(NC):
        for m in range(1, NY):
            o_copy(c, m).wait_send()


def on_device(
    tokens,
    routes,
    route_weights,
    domains,
    gate_weight,
    up_weight,
    down_weight,
    up_entry,
    up_exit,
    down_entry,
    down_exit,
):
    facts = jnp.concatenate(
        [
            jnp.transpose(routes.reshape(BLOCK, TOP)).astype(F32),
            jnp.transpose(route_weights.reshape(BLOCK, TOP)),
            domains.reshape(1, BLOCK).astype(F32),
        ]
    )
    facts = jnp.pad(facts, ((0, 16 - 2 * TOP - 1), (0, 128 - BLOCK)))

    any_spec = pl.BlockSpec(memory_space=pl.ANY)
    vmem_spec = pl.BlockSpec(memory_space=pltpu.VMEM)
    dma = pltpu.SemaphoreType.DMA
    vmem = pltpu.VMEM
    return pl.pallas_call(
        kernel,
        out_shape=jax.ShapeDtypeStruct((STEPS, TOK, PART), BF16),
        in_specs=[any_spec, vmem_spec] + [any_spec] * 3 + [vmem_spec] * 4,
        out_specs=vmem_spec,
        scratch_shapes=[
            [vmem((8, wide, 2 * FFL), BF16) for _, wide in OWN],
            vmem((FFL, D), BF16),
            vmem((NC, NY, 128, W), BF16),
            vmem((NY, 2 * NZ, 128), F32),
            vmem((NY, 2 * NZ, 128), F32),
            vmem((NZ * PAD, NY * 128), BF16),
            vmem((NY * 128, NZ * 128), BF16),
            vmem((NC, NZ, PAD, W), BF16),
            vmem((NC, NZ, PAD, W), BF16),
            [vmem((ALL, 8 * wide), BF16) for _, wide in OWN],
            vmem((ALL, LOW), BF16),
            vmem((ALL, 2 * FFL), F32),
            vmem((ALL, FFL), BF16),
            vmem((2, ALL, LOW), BF16),
            vmem((2, NH, QUART, LOW), BF16),
            vmem((2, NH, NX, QUART, LOW), BF16),
            vmem((2, ALL, LOW), BF16),
            vmem((NC, NX, ALL, WIDE), BF16),
            vmem((NC, NX, ALL, WIDE), BF16),
            vmem((NC, NH, 3, HALF, WIDE), BF16),
            vmem((NC, NH, 2, QUART, WIDE), BF16),
            vmem((NC, NH, 2, HALF, WIDE), BF16),
            vmem((NC, NZ, PAD, WIDE), BF16),
            vmem((NC, NZ, 128, WIDE), BF16),
            vmem((NC, BLOCK, WIDE), F32),
            vmem((NC, NY, BLOCK, WIDE), BF16),
            vmem((NC, NY, BLOCK, WIDE), BF16),
            dma((4 * NC + 1,)),
            dma((NY,)), dma((NY,)),
            dma((NC * NY,)), dma((NC * NY,)),
            dma((NC * NZ,)), dma((NC * NZ,)),
            dma((NC * NH * 8,)), dma((NC * NH * 8,)),
            dma((NH * 16,)), dma((NH * 16,)),
            dma((NC * NH * NX,)), dma((NC * NH * NX,)),
            dma((NC * NH * 2,)), dma((NC * NH * 2,)),
            dma((NC * NH * 2,)), dma((NC * NH * 2,)),
            dma((NC * NZ,)), dma((NC * NZ,)),
            dma((NC * NY,)), dma((NC * NY,)),
        ],
        compiler_params=pltpu.CompilerParams(
            collective_id=0, has_side_effects=True, vmem_limit_bytes=62 * 1024 * 1024
        ),
        name="moe",
    )(
        tokens, facts,
        gate_weight[0].reshape(8, PART, FFL), up_weight[0].reshape(8, PART, FFL), down_weight[0],
        up_entry[0], up_exit[0], down_entry[0], down_exit[0],
    )


def solution(mesh):
    in_specs = (
        P(None, "expert", None),
        P(None, "expert", None),
        P(None, "expert", None),
        P(None, "expert"),
        P("expert", None, "dp"),
        P("expert", None, "dp"),
        P("expert", "dp", None),
        P("expert", "dp", None),
        P("expert", None, "dp"),
        P("expert", "dp", None),
        P("expert", None, "dp"),
    )
    out_specs = P(None, "expert", "dp")
    return jax.shard_map(
        on_device, mesh=mesh, in_specs=in_specs, out_specs=out_specs, check_vma=False
    )
```

time: 682 us -> 121 us (0.18)
  waiting for transfers between devices: 500 us -> 0 us
  Pallas kernels: 0 us -> 115 us
  starting transfers between devices: 55.2 us -> 0 us
  local copies, waits for them, and re-layouts: 55.3 us -> 2.55 us
  matrix products: 43.2 us -> 0 us
  between operations: 13.6 us -> 0.01 us
  other arithmetic: 11.9 us -> 1.98 us
    all_to_all x6 -> x0, waiting for transfers between devices: 322 us -> none  [the longest x2 298 us: on_device(): lax.all_to_all(send_rows, 'expert', split_axis=0, concat_axis=0, tiled=True)]
    psum x2 -> x0, waiting for transfers between devices: 116 us -> none  [the longest x1 61 us: on_device(): lax.psum(jnp.dot(own_columns, up_enter, preferred_element_type=jnp.float3...]
    pallas_call x0 -> x1, Pallas kernels: none -> 115 us  [on_device(): pl.pallas_call(kernel, out_shape=jax.ShapeDtypeStruct((STEPS, TOK, PART),...]
    unnamed x6 -> x0, waiting for transfers between devices: 61.2 us -> none
    all_to_all x6 -> x0, starting transfers between devices: 54.9 us -> none  [the longest x2 20.1 us: on_device(): lax.all_to_all(summed.reshape(experts, capacity, part_width).astype(jnp.b...]
    dot_general x18 -> x0, matrix products: 43.2 us -> none  [the longest x2 9.73 us: on_device(): jnp.dot(hidden, down_local, preferred_element_type=jnp.float32)]
    reshape x10 -> x1, local copies, waits for them, and re-layouts: 27.4 us -> 0.08 us  [on_device(): route_weights.reshape(BLOCK, TOP)]
    unnamed x26 -> x2, local copies, waits for them, and re-layouts: 18.7 us -> 2.29 us
  transfers between devices with their start and end apart: 10 -> 0, of which waited for: 8 -> 0; matrix products, arithmetic and copies ran while one was open for 10% -> 0% of each run, Pallas kernels for 0% -> 0%
where the time goes in v2:
time: 121 us; the launch traced here: 119 us
  Pallas kernels  115 us (95%)
  local copies, waits for them, and re-layouts  2.55 us (2%)
  other arithmetic  1.98 us (2%)
    pallas_call x1, Pallas kernels, on_device(): pl.pallas_call(kernel, out_shape=jax.ShapeDtypeStruct((STEPS, TOK, PART),...  115 us

profile of v2, /device:TPU:40, one launch (start us, length us, event | category | flops | bytes accessed | tf_op | source)
XLA Modules:
  0.0 119.4 jit_solution(15382958305137811433)
XLA Ops:
  0.0 0.7 convert_element_type.28
  0.7 0.1 convert_element_type.29
  0.8 0.7 convert_element_type.25
  1.5 0.1 convert_element_type.26
  1.5 0.7 copy.13
  2.2 0.1 reshape.19
  2.3 0.6 select_maximum_fusion.facts
  2.9 114.9 %moe.1 = bf16[2,48,896]{2,1,0:T(8,128)(2,1)} custom-call(bf16[2,48,7168]{2,1,0:T(8,128)(2,1)} %tokens.1, f32[16,128]{1,0:T(8,128)} %select_maximum_fusion.facts, bf16[8,896,256]{2,1,0:T(8,128)(2,1)} %bitcast.13, bf16[8,896,256]{2,1,0:T(8,128)(2,1)} %bitcast.14, bf16[256,7168]{1,0:T(8,128)(2,1)} %bitcast.15, bf16[896,128]{1,0:T(8,128)(2,1)} %bitcast.16, ...), custom_call_target="tpu_custom_call" | custom-call | tf_op jit(solution)/shard_map/moe/pallas_call | solution.py:508
  117.8 1.6 %copy.15 = bf16[2,48,896]{2,1,0:T(8,128)(2,1)} copy(bf16[2,48,896]{2,1,0:T(8,128)(2,1)} %moe.1) | data formatting | bytes 344064
  (1 shorter events, 0.0 us)

commit v3 on v2

--- a/solution.py
+++ b/solution.py
@@ -36,17 +36,17 @@
 QUART = HALF // 2
 
 ORDER = (
-    "y4", "y6", "y1", "y3", "y0", "y5", "y2", "T", "B4", "B6", "B1", "B3", "b1", "b3", "b6", "b4", "B0", "B5", "B2",
-    "C4.0", "b5", "b0", "b2", "C6.0", "C1.0", "D4.0", "C3.0", "C1.1", "D6.0", "C3.1", "D1.0", "e4.0", "C6.1", "E4.0",
-    "D3.0", "C4.1", "D1.1", "e6.0", "E6.0", "D3.1", "e1.0", "C0.0", "E1.0", "D6.1", "C5.0", "e3.0", "E3.0", "D4.1",
-    "C2.0", "L1.0", "e3.1", "e1.1", "C5.1", "L2.0", "D0.0", "E3.1", "e6.1", "E1.1", "E6.1", "D5.0", "e4.1", "C0.1",
-    "E4.1", "D2.0", "C2.1", "L1.1", "D5.1", "L2.1", "L3.0", "e0.0", "e5.0", "E0.0", "E5.0", "D0.1", "e2.0", "E2.0",
-    "H.0", "D2.1", "M1.0", "P6.0", "P0.0", "M2.0", "P3.0", "Q6.0", "Q0.0", "P1.0", "Q3.0", "P4.0", "P5.0", "Q1.0",
-    "P2.0", "Q4.0", "Q5.0", "L3.1", "e5.1", "Q2.0", "e2.1", "R6.0", "M3.0", "R0.0", "e0.1", "E5.1", "R3.0", "R1.0",
-    "R4.0", "E0.1", "R5.0", "R2.0", "E2.1", "H.1", "S6.0", "M1.1", "P5.1", "S0.0", "M2.1", "P3.1", "S3.0", "Q5.1",
-    "P2.1", "Q3.1", "S1.0", "P4.1", "Q2.1", "P1.1", "S4.0", "Q4.1", "P6.1", "S5.0", "Q1.1", "P0.1", "Q6.1", "S2.0",
-    "Q0.1", "M3.1", "R5.1", "R3.1", "R2.1", "R4.1", "R1.1", "R6.1", "R0.1", "S5.1", "S3.1", "S2.1", "S4.1", "S1.1",
-    "U5", "S6.1", "U3", "S0.1", "U2", "U4", "V5", "U1", "V3", "U6", "V2", "U0", "V4", "V1", "V6", "V0",
+    "y0", "y1", "y2", "y3", "y4", "y5", "G1", "y6", "T", "B0", "B1", "B2", "b0", "B3", "G2", "B4", "B5", "B6", "b1",
+    "b2", "b3", "b4", "b5", "b6", "C0.0", "G3", "C1.0", "C2.0", "D0.0", "C0.1", "D1.0", "D2.0", "C3.0", "e0.0",
+    "C4.0", "E0.0", "D0.1", "e1.0", "C5.0", "e2.0", "E1.0", "C6.0", "D3.0", "E2.0", "C1.1", "D4.0", "C2.1", "e0.1",
+    "D5.0", "C3.1", "E0.1", "D6.0", "C4.1", "e3.0", "C5.1", "D1.1", "E3.0", "e4.0", "C6.1", "D2.1", "E4.0", "e5.0",
+    "E5.0", "D3.1", "e6.0", "E6.0", "D4.1", "H.0", "M1.0", "D5.1", "P1.0", "M2.0", "P5.0", "P6.0", "D6.1", "Q1.0",
+    "Q5.0", "P4.0", "Q6.0", "P2.0", "P0.0", "Q4.0", "P3.0", "Q2.0", "Q0.0", "e1.1", "e2.1", "Q3.0", "e3.1", "e4.1",
+    "E1.1", "M3.0", "R1.0", "E2.1", "R5.0", "R6.0", "E3.1", "R4.0", "R2.0", "e5.1", "R0.0", "E4.1", "R3.0", "e6.1",
+    "E5.1", "S1.0", "E6.1", "H.1", "M1.1", "S5.0", "P1.1", "M2.1", "S6.0", "P5.1", "S4.0", "Q1.1", "P6.1", "S2.0",
+    "Q5.1", "P4.1", "Q6.1", "S0.0", "P2.1", "Q4.1", "P0.1", "S3.0", "Q2.1", "P3.1", "Q0.1", "M3.1", "R1.1", "Q3.1",
+    "R5.1", "R6.1", "R4.1", "R2.1", "R0.1", "S1.1", "R3.1", "S5.1", "S6.1", "S4.1", "S2.1", "U1", "S0.1", "S3.1",
+    "U5", "U6", "U4", "V1", "U2", "U0", "V5", "U3", "V6", "V4", "V2", "V0", "V3",
 )
 
 
@@ -55,11 +55,11 @@
 
 
 def kernel(
-    tokens, facts, gate, up, down, up_enter, up_leave, down_enter, down_leave,
+    tokens, routes, route_weights, domains, gate, up, down, up_enter, up_leave, down_enter, down_leave,
     out,
-    ws, wd, g, table, tab, sel, selwt, zs, zr, xs, mask, acc, hid,
+    ws, ent, wd, g, raw, table, tab, sel, selwt, zs, zr, xs, mask, acc, accl, hid,
     lp, lq, lx, lf, sb, sr, ss, hr, tr, tp, vz, own, ys, yr,
-    load_sem, tsend, trecv, ysend, yrecv, zsend, zrecv, xsend, xrecv,
+    load_sem, esend, erecv, tsend, trecv, ysend, yrecv, zsend, zrecv, xsend, xrecv,
     lsend, lrecv, bsend, brecv, hsend, hrecv, rsend, rrecv, vsend, vrecv, osend, orecv,
 ):
     dp = lax.axis_index("dp")
@@ -109,10 +109,13 @@
     for c, (off, wide) in enumerate(OWN):
         for half, array in ((0, gate), (1, up)):
             cols = pl.ds(half * FFL, FFL)
-            loads.append((array.at[:, pl.ds(off, wide), :], ws[c].at[:, :, cols]))
+            for side in range(2):
+                rows = array.at[:, side, pl.ds(off, wide), :]
+                loads.append((rows, ws[c].at[pl.ds(side * NX, NX), :, cols]))
     loads.append((down, wd))
     loads = [pltpu.make_async_copy(a, b, load_sem.at[i]) for i, (a, b) in enumerate(loads)]
-    for copy in loads:
+    enter_load = pltpu.make_async_copy(up_enter, ent.at[core * NX + x], load_sem.at[len(loads)])
+    for copy in loads[:n_tokens] + [enter_load] + loads[n_tokens:]:
         copy.start()
     for c in range(NC):
         for m in range(NY):
@@ -122,6 +125,12 @@
     def count(shape, dim):
         return lax.broadcasted_iota(jnp.int32, shape, dim)
 
+    raw[...] = jnp.zeros_like(raw)
+    for s in range(STEPS):
+        raw[s * TOK : (s + 1) * TOK, :TOP] = routes[s].astype(F32)
+        raw[s * TOK : (s + 1) * TOK, TOP : 2 * TOP] = route_weights[s]
+    facts = raw[...].T
+    of_token = jnp.concatenate([domains[s : s + 1, :].astype(F32) for s in range(STEPS)], axis=1)
     row, token = count((EXPERTS, 128), 0), count((EXPERTS, 128), 1)
     expert = ((row % NZ) * NY + row // NZ).astype(F32)
     hit, weight = jnp.zeros((EXPERTS, 128), F32), jnp.zeros((EXPERTS, 128), F32)
@@ -135,7 +144,8 @@
     code = jnp.where(hit > 0.0, rank + jnp.where(token >= TOK, float(CAP), 0.0), -1.0)
     table[:, :NZ, :] = code.reshape(NY, NZ, 128)
     table[:, NZ:, :] = weight.reshape(NY, NZ, 128)
-    domain = facts[2 * TOP : 2 * TOP + 1, :] == (first // RANK).astype(F32)
+    of_token = jnp.concatenate([of_token, jnp.zeros((1, 128 - BLOCK), F32)], axis=1)
+    domain = of_token == (first // RANK).astype(F32)
     g[0, 0, :BLOCK, 128:] = jnp.where(domain, 1.0, 0.0).T[:BLOCK].astype(BF16)
     pl.semaphore_wait(barrier, 14)
 
@@ -201,15 +211,21 @@
         for n in of_half(1):
             z_copy(c, n).start()
 
-    def near(c, h, kind, to, who):
-        n = (c * NH + h) * 8 + kind
-        block = xs[c].at[pl.ds(h * HALF, HALF), lanes(who, OWN[c][1])]
+    def near(c, h, kind, to, whose):
+        n = (c * NH + h) * 5 + kind
+        block = xs[c].at[pl.ds(h * HALF, HALF), lanes(core * NX + whose, OWN[c][1])]
         return send(block, block, xsend.at[n], xrecv.at[n], dp=to)
 
-    def far(c, h, kind, to, who):
-        n = (c * NH + h) * 8 + kind
-        block = xs[c].at[pl.ds(h * HALF + (kind - 3) * QUART, QUART), lanes(who, OWN[c][1])]
+    def far(c, h, kind, to, whose):
+        n = (c * NH + h) * 5 + kind
+        rows = pl.ds(h * HALF + (kind - 2) * QUART, QUART)
+        block = xs[c].at[rows, lanes(core * NX + whose, OWN[c][1])]
         return send(block, block, xsend.at[n], xrecv.at[n], dp=to)
+
+    def cross(c, h, side):
+        n = (c * NH + h) * 5 + 4
+        block = xs[c].at[pl.ds(h * HALF, HALF), lanes(side, NX * OWN[c][1])]
+        return send(block, block, xsend.at[n], xrecv.at[n], dp=sib)
 
     def stage_c(c, h):
         for n in of_half(h):
@@ -218,43 +234,70 @@
         take = W if c == 0 else wide
         rows = zr[c, 4 * h : 4 * h + 4, :, :take].astype(F32)[:, :ROWS]
         rows = rows.reshape(HALF, take).astype(BF16)
-        xs[c][mine, lanes(dp, wide)] = rows[:, :wide]
+        xs[c][mine, lanes(core * NX + x, wide)] = rows[:, :wide]
         if c == 0:
             mask[mine, :] = rows[:, 128:]
-        near(c, h, 0, xp, dp).start()
-        near(c, h, 1, xm, dp).start()
-        near(c, h, 2, sib, dp).start()
+        near(c, h, 0, xp, x).start()
+        near(c, h, 1, xm, x).start()
 
     def stage_d(c, h):
-        near(c, h, 0, xp, xm).wait_recv()
-        far(c, h, 3, xp, xm).start()
-        near(c, h, 5, sib, xm).start()
-        near(c, h, 1, xm, xp).wait_recv()
-        far(c, h, 4, xm, xp).start()
-        near(c, h, 6, sib, xp).start()
+        near(c, h, 0, xp, im).wait_recv()
+        far(c, h, 2, xp, im).start()
+        near(c, h, 1, xm, ip).wait_recv()
+        far(c, h, 3, xm, ip).start()
 
     started = [False] * NH
 
     def stage_e(c, h):
-        far(c, h, 3, xp, xo).wait_recv()
-        far(c, h, 4, xm, xo).wait_recv()
-        near(c, h, 7, sib, xo).start()
+        far(c, h, 2, xp, io).wait_recv()
+        far(c, h, 3, xm, io).wait_recv()
+        cross(c, h, core).start()
 
     loaded = set()
 
+    def enter_copy(kind, to, whose):
+        rows = pl.ds(0, PART) if kind < 2 else pl.ds((kind - 2) * (PART // 2), PART // 2)
+        block = ent.at[core * NX + whose, rows]
+        return send(block, block, esend.at[kind], erecv.at[kind], dp=to)
+
+    def enter_cross(side):
+        block = ent.at[pl.ds(side * NX, NX)]
+        return send(block, block, esend.at[4], erecv.at[4], dp=sib)
+
+    def stage_g(s):
+        if s == 1:
+            enter_load.wait()
+            enter_copy(0, xp, x).start()
+            enter_copy(1, xm, x).start()
+        elif s == 2:
+            enter_copy(0, xp, im).wait_recv()
+            enter_copy(2, xp, im).start()
+            enter_copy(1, xm, ip).wait_recv()
+            enter_copy(3, xm, ip).start()
+        else:
+            enter_copy(2, xp, io).wait_recv()
+            enter_copy(3, xm, io).wait_recv()
+            enter_cross(core).start()
+
     def stage_e2(c, h):
-        for kind, step in ((2, 0), (5, 3), (6, 1), (7, 2)):
-            near(c, h, kind, sib, ((x + step) % NX) * 2 + 1 - core).wait_recv()
+        cross(c, h, 1 - core).wait_recv()
+        if "enter" not in loaded:
+            loaded.add("enter")
+            enter_cross(1 - core).wait_recv()
         if c not in loaded:
             loaded.add(c)
-            for half in range(2):
-                loads[n_tokens + c * 2 + half].wait()
+            for n in range(4):
+                loads[n_tokens + c * 4 + n].wait()
         mine, wide = slice(h * HALF, (h + 1) * HALF), OWN[c][1]
         term = dot(xs[c][mine, :], ws[c][...].reshape(8 * wide, 2 * FFL))
+        off = OWN[c][0]
+        low = dot(xs[c][mine, :], ent[:, off : off + wide, :].reshape(8 * wide, LOW))
         if started[h]:
             acc[mine, :] += term
+            accl[mine, :] += low
         else:
             acc[mine, :] = term
+            accl[mine, :] = low
             started[h] = True
 
     def pair_copy(q, h):
@@ -275,13 +318,7 @@
         mine = slice(h * HALF, (h + 1) * HALF)
         home = pl.ds(pl.multiple_of(h * HALF + core * QUART, 16), QUART)
         if s == 1:
-            if q == 0:
-                total = jnp.zeros((HALF, LOW), F32)
-                for c, (off, wide) in enumerate(OWN):
-                    block = xs[c][mine, lanes(dp, wide)]
-                    total += dot(block, up_enter[off : off + wide, :])
-            else:
-                total = dot(hid[mine, :], down_enter[...])
+            total = dot(hid[mine, :], down_enter[...])
             lp[q, mine, :] = total.astype(BF16)
             pair_copy(q, h).start()
         elif s == 2:
@@ -299,9 +336,9 @@
 
     def stage_hidden(h):
         mine = slice(h * HALF, (h + 1) * HALF)
-        back_copy(0, h, 1 - core).wait_recv()
         gated = acc[mine, :FFL]
-        upped = acc[mine, FFL:] + dot(lf[0, mine, :], up_leave[...])
+        low = (accl[mine, :] * mask[mine, :].astype(F32)).astype(BF16)
+        upped = acc[mine, FFL:] + dot(low, up_leave[...])
         hid[mine, :] = (gated / (1.0 + jnp.exp(-gated)) * upped).astype(BF16)
         if "down" not in loaded:
             loaded.add("down")
@@ -312,15 +349,14 @@
         cols = pl.ds(pl.multiple_of(shard * PART + off, 128), wide)
         return dot(hid[h * HALF : (h + 1) * HALF, :], wd[:, cols])
 
-    def b_copy(c, h, i):
-        cols, n = pl.ds(0, OWN[c][1]), (c * NH + h) * NX + i
+    def b_copy(c, h):
+        cols, n = pl.ds(0, OWN[c][1]), c * NH + h
         rows = pl.ds(h * HALF, HALF)
         return send(
-            sb.at[c, i, rows, cols], sr.at[c, i, rows, cols], bsend.at[n], brecv.at[n], dp=sib
+            sb.at[c, :, rows, cols], sr.at[c, :, rows, cols], bsend.at[n], brecv.at[n], dp=sib
         )
 
     def paired(c, h, i):
-        b_copy(c, h, i).wait_recv()
         more = sr[c, i, h * HALF : (h + 1) * HALF, : OWN[c][1]].astype(F32)
         return partial(c, h, i * 2 + core) + more
 
@@ -355,16 +391,16 @@
     def stage_1(c, h):
         wide = OWN[c][1]
 
-        def one(j, carry):
-            i = (x + 2 + j) % NX
+        def one(i, carry):
             term = partial(c, h, i * 2 + 1 - core)
             sb[c, i, h * HALF : (h + 1) * HALF, :wide] = term.astype(BF16)
-            b_copy(c, h, i).start()
             return carry
 
         lax.fori_loop(0, NX, one, 0)
+        b_copy(c, h).start()
 
     def stage_2(c, h):
+        b_copy(c, h).wait_recv()
         ss[c, h, 2, :, : OWN[c][1]] = paired(c, h, io).astype(BF16)
         h_copy(c, h, 0).start()
         h_copy(c, h, 1).start()
@@ -387,9 +423,9 @@
         off, wide = OWN[c]
         if ("low", h) not in loaded:
             loaded.add(("low", h))
-            back_copy(1, h, 1 - core).wait_recv()
+            back_copy(0, h, 1 - core).wait_recv()
         total = paired(c, h, x)
-        total += dot(lf[1, h * HALF : (h + 1) * HALF, :], down_leave[:, off : off + wide])
+        total += dot(lf[0, h * HALF : (h + 1) * HALF, :], down_leave[:, off : off + wide])
         for i in range(2):
             r_copy(c, h, i).wait_recv()
             total += tr[c, h, i, :, :wide].astype(F32)
@@ -428,7 +464,7 @@
     tab[0] = table[y]
     stages = {
         "T": stage_tables, "y": stage_y, "B": stage_b, "b": stage_b2, "C": stage_c, "D": stage_d,
-        "e": stage_e, "E": stage_e2, "H": stage_hidden, "P": stage_1, "Q": stage_2, "R": stage_3,
+        "G": stage_g, "e": stage_e, "E": stage_e2, "H": stage_hidden, "P": stage_1, "Q": stage_2, "R": stage_3,
         "S": stage_4, "U": stage_5, "V": stage_6,
     }
     def sent_out(c):
@@ -437,43 +473,41 @@
         for n in range(1, NZ):
             z_copy(c, n).wait_send()
         for h in range(NH):
-            for kind in (0, 1, 2, 5, 6, 7):
-                near(c, h, kind, sib, dp).wait_send()
             for i in range(2):
-                far(c, h, 3 + i, xp, dp).wait_send()
-
-    def sent_back():
-        for m in range(1, NY):
-            table_copy(m).wait_send()
-        for h in range(NH):
-            for q in range(2):
-                pair_copy(q, h).wait_send()
-                back_copy(q, h, core).wait_send()
-                for j in range(1, NX):
-                    low_copy(q, h, j).wait_send()
-            for c in range(NC):
-                for i in range(2):
-                    h_copy(c, h, i).wait_send()
-                    r_copy(c, h, i).wait_send()
-                for i in range(NX):
-                    b_copy(c, h, i).wait_send()
-        for c in range(NC):
-            for n in range(1, NZ):
-                v_copy(c, n).wait_send()
-
-    mixes = 0
+                near(c, h, i, xp, x).wait_send()
+                far(c, h, 2 + i, xp, x).wait_send()
+                h_copy(c, h, i).wait_send()
+            cross(c, h, core).wait_send()
+            b_copy(c, h).wait_send()
+
+    def sent_back(c, h):
+        for i in range(2):
+            r_copy(c, h, i).wait_send()
+        for n in of_half(h):
+            v_copy(c, n).wait_send()
+
     for name in ORDER:
-        if name[0] == "U":
-            sent_out(mixes)
-            mixes += 1
-            if mixes == NC:
-                sent_back()
         numbers = [int(n) for n in name[1:].split(".") if n]
-        if name[0] in "LM":
-            stage_low(numbers[0], "LM".index(name[0]), numbers[1])
+        if name[0] == "M":
+            stage_low(numbers[0], 0, numbers[1])
         else:
+            if name[0] == "S" and numbers[1] == 1:
+                sent_out(numbers[0])
+                sent_back(numbers[0], 0)
             stages[name[0]](*numbers)
-
+            if name[0] == "V":
+                sent_back(numbers[0], 1)
+
+    for kind in range(4):
+        enter_copy(kind, xp, x).wait_send()
+    enter_cross(core).wait_send()
+    for m in range(1, NY):
+        table_copy(m).wait_send()
+    for h in range(NH):
+        pair_copy(0, h).wait_send()
+        back_copy(0, h, core).wait_send()
+        for j in range(1, NX):
+            low_copy(0, h, j).wait_send()
     for c in range(NC):
         for m in range(1, NY):
             o_copy(c, m).wait_send()
@@ -492,15 +526,6 @@
     down_entry,
     down_exit,
 ):
-    facts = jnp.concatenate(
-        [
-            jnp.transpose(routes.reshape(BLOCK, TOP)).astype(F32),
-            jnp.transpose(route_weights.reshape(BLOCK, TOP)),
-            domains.reshape(1, BLOCK).astype(F32),
-        ]
-    )
-    facts = jnp.pad(facts, ((0, 16 - 2 * TOP - 1), (0, 128 - BLOCK)))
-
     any_spec = pl.BlockSpec(memory_space=pl.ANY)
     vmem_spec = pl.BlockSpec(memory_space=pltpu.VMEM)
     dma = pltpu.SemaphoreType.DMA
@@ -508,12 +533,14 @@
     return pl.pallas_call(
         kernel,
         out_shape=jax.ShapeDtypeStruct((STEPS, TOK, PART), BF16),
-        in_specs=[any_spec, vmem_spec] + [any_spec] * 3 + [vmem_spec] * 4,
+        in_specs=[any_spec] + [vmem_spec] * 3 + [any_spec] * 4 + [vmem_spec] * 3,
         out_specs=vmem_spec,
         scratch_shapes=[
             [vmem((8, wide, 2 * FFL), BF16) for _, wide in OWN],
+            vmem((2 * NX, PART, LOW), BF16),
             vmem((FFL, D), BF16),
             vmem((NC, NY, 128, W), BF16),
+            vmem((128, 128), F32),
             vmem((NY, 2 * NZ, 128), F32),
             vmem((NY, 2 * NZ, 128), F32),
             vmem((NZ * PAD, NY * 128), BF16),
@@ -523,11 +550,12 @@
             [vmem((ALL, 8 * wide), BF16) for _, wide in OWN],
             vmem((ALL, LOW), BF16),
             vmem((ALL, 2 * FFL), F32),
+            vmem((ALL, LOW), F32),
             vmem((ALL, FFL), BF16),
-            vmem((2, ALL, LOW), BF16),
-            vmem((2, NH, QUART, LOW), BF16),
-            vmem((2, NH, NX, QUART, LOW), BF16),
-            vmem((2, ALL, LOW), BF16),
+            vmem((1, ALL, LOW), BF16),
+            vmem((1, NH, QUART, LOW), BF16),
+            vmem((1, NH, NX, QUART, LOW), BF16),
+            vmem((1, ALL, LOW), BF16),
             vmem((NC, NX, ALL, WIDE), BF16),
             vmem((NC, NX, ALL, WIDE), BF16),
             vmem((NC, NH, 3, HALF, WIDE), BF16),
@@ -538,13 +566,14 @@
             vmem((NC, BLOCK, WIDE), F32),
             vmem((NC, NY, BLOCK, WIDE), BF16),
             vmem((NC, NY, BLOCK, WIDE), BF16),
-            dma((4 * NC + 1,)),
+            dma((6 * NC + 2,)),
+            dma((5,)), dma((5,)),
             dma((NY,)), dma((NY,)),
             dma((NC * NY,)), dma((NC * NY,)),
             dma((NC * NZ,)), dma((NC * NZ,)),
-            dma((NC * NH * 8,)), dma((NC * NH * 8,)),
-            dma((NH * 16,)), dma((NH * 16,)),
-            dma((NC * NH * NX,)), dma((NC * NH * NX,)),
+            dma((NC * NH * 5,)), dma((NC * NH * 5,)),
+            dma((NH * 8,)), dma((NH * 8,)),
+            dma((NC * NH,)), dma((NC * NH,)),
             dma((NC * NH * 2,)), dma((NC * NH * 2,)),
             dma((NC * NH * 2,)), dma((NC * NH * 2,)),
             dma((NC * NZ,)), dma((NC * NZ,)),
@@ -555,8 +584,8 @@
         ),
         name="moe",
     )(
-        tokens, facts,
-        gate_weight[0].reshape(8, PART, FFL), up_weight[0].reshape(8, PART, FFL), down_weight[0],
+        tokens, routes, route_weights, domains,
+        gate_weight[0].reshape(NX, 2, PART, FFL), up_weight[0].reshape(NX, 2, PART, FFL), down_weight[0],
         up_entry[0], up_exit[0], down_entry[0], down_exit[0],
     )
 

time: 121 us -> 118 us (0.975)
  Pallas kernels: 115 us -> 113 us
  other arithmetic: 1.98 us -> 0 us
  local copies, waits for them, and re-layouts: 2.55 us -> 4.4 us
    unnamed x2 -> x3, local copies, waits for them, and re-layouts: 2.29 us -> 4.4 us
    pallas_call x1, Pallas kernels: 115 us -> 113 us  [on_device(): pl.pallas_call(kernel, out_shape=jax.ShapeDtypeStruct((STEPS, TOK, PART),...]
    convert_element_type x2 -> x0, other arithmetic: 1.37 us -> none  [the longest x1 0.69 us: on_device(): jnp.transpose(routes.reshape(BLOCK, TOP)).astype(F32)]
where the time goes in v3:
time: 118 us; the launch traced here: 117 us
  Pallas kernels  113 us (96%)
  local copies, waits for them, and re-layouts  4.4 us (4%)
    pallas_call x1, Pallas kernels, on_device(): pl.pallas_call(kernel, out_shape=jax.ShapeDtypeStruct((STEPS, TOK, PART),...  113 us
    unnamed x3, local copies, waits for them, and re-layouts  4.4 us

profile of v3, /device:TPU:40, one launch (start us, length us, event | category | flops | bytes accessed | tf_op | source)
XLA Modules:
  0.0 117.3 jit_solution(15744848914148462769)
XLA Ops:
  0.0 1.4 %copy.12.routes = s32[2,48,4]{2,1,0:T(8,128)} copy(s32[2,48,4]{1,2,0:T(4,128)} %param.12) | data formatting | bytes 3072 | tf_op args[1]
  1.4 1.4 %copy.13.route_weights = f32[2,48,4]{2,1,0:T(8,128)} copy(f32[2,48,4]{1,2,0:T(4,128)} %param.13) | data formatting | bytes 3072 | tf_op args[2]
  2.8 112.9 %moe.1 = bf16[2,48,896]{2,1,0:T(8,128)(2,1)} custom-call(bf16[2,48,7168]{2,1,0:T(8,128)(2,1)} %tokens.1, s32[2,48,4]{2,1,0:T(8,128)} %copy.12.routes, f32[2,48,4]{2,1,0:T(8,128)} %copy.13.route_weights, s32[2,48]{1,0:T(2,128)} %domains.1, bf16[4,2,896,256]{3,2,1,0:T(8,128)(2,1)} %bitcast.7, bf16[4,2,896,256]{3,2,1,0:T(8,128)(2,1)} %bitcast.8, ...), custom_call_target="tpu_custom_call" | custom-call | tf_op jit(solution)/shard_map/moe/pallas_call | solution.py:533
  115.7 1.6 %copy.15 = bf16[2,48,896]{2,1,0:T(8,128)(2,1)} copy(bf16[2,48,896]{2,1,0:T(8,128)(2,1)} %moe.1) | data formatting | bytes 344064
